TPU v7x, 256 devices: a whole 4x4x8 slice. The times are simulated.
256 devices in a mesh: rep: 64 (over z, x, core), tp: 4 (over y).
Axes of the slice: x: 4, y: 4, z: 8, core: 2. Of those that a mesh axis runs over, the one named last changes fastest.
Arguments:
- normed_input_rows: bfloat16 [65536, 8192], P('rep', 'tp'), may hold values from -6 to 6
- key_projection_weight: bfloat16 [8192, 512], P('tp'), may hold values from -0.0625 to 0.0625
- value_projection_weight: bfloat16 [8192, 512], P('tp'), may hold values from -0.0625 to 0.0625
- adapter_down_factors: bfloat16 [256, 8192, 64], P('rep', 'tp'), may hold values from -0.0625 to 0.0625
- adapter_up_factors: bfloat16 [256, 64, 2, 512], P('rep', None, None, 'tp'), may hold values from -0.75 to 0.75
- request_owner_replica: int32 [4096, 1], P('rep'), may hold values from 0 to 63; in each aligned block of 64 rows (0 to 63, 64 to 127, ...) at most 2 rows name the same one
- request_adapter_slot: int32 [4096], P('rep'), may hold values from 0 to 3
- prefill_adapter_slot: int32 [64], P('rep'), may hold values from 0 to 3
- prefill_first_row: int32 [64], P('rep'), may hold values from 0 to 4095
- context_length: int32 [4096], P('rep'), may hold values from 2 to 64, as said below
- request_page_table: int32 [4096, 4], P('rep'), may hold values from 0 to 255, as said below
- queries: bfloat16 [4096, 4096], P('rep', 'tp'), may hold values from -48 to 48
- rotated_cache_keys: bfloat16 [16384, 16, 512], P('rep', None, 'tp'), may hold values from -16 to 16
- paged_cache_values: bfloat16 [16384, 16, 512], P('rep', None, 'tp'), may hold values from -6 to 6
Outputs:
- decode_kv: bfloat16 [4096, 2, 512], P('rep', None, 'tp')
- prefill_kv: bfloat16 [61440, 2, 512], P('rep', None, 'tp')
- attended: bfloat16 [4096, 4096], P('rep', 'tp')
Inputs may be any that keep to these rules, and one draw needn't show every extreme that they name: `request_owner_replica`: among the 64 decode requests of one replica at most 2 have adapters held by one owner, and some owner holds exactly 2 of them. `context_length`: every replica has a decode request with exactly 64 cached positions. `request_page_table`: pages may be shared between requests.
All inputs are finite; a program needn't handle non-finite values.
Results may differ from a plain program's by a relative error of at most 0.0075.
Values may be sent and summed in bfloat16 or wider, within the bound.
A program may use at most 128 MiB of HBM per device.

v0:
```python
import jax
import jax.numpy as jnp
from jax import lax
from jax.sharding import PartitionSpec as P

HEAD_WIDTH = 128


rope_base = 500000.0
highest_precision = lax.Precision.HIGHEST


def rotate_heads(values, positions):
    row_count = values.shape[0]
    head_rows = values.reshape(row_count, -1, HEAD_WIDTH)
    half_size = HEAD_WIDTH // 2
    freq_index = jnp.arange(half_size).astype(jnp.float32)
    frequency = rope_base ** (-2.0 * freq_index / HEAD_WIDTH)
    angles = positions.astype(jnp.float32)[:, None] * frequency[None, :]
    cosine = jnp.cos(angles)[:, None, :]
    sine_part = jnp.sin(angles)[:, None, :]
    first_half = head_rows[..., :half_size]
    second_half = head_rows[..., half_size:]
    turned = jnp.concatenate(
        [
            first_half * cosine - second_half * sine_part,
            second_half * cosine + first_half * sine_part,
        ],
        axis=-1,
    )
    return turned.reshape(row_count, -1)


def attend(queries, new_keys, new_values, cached_keys, cached_values, lengths):
    requests, span_len, columns = cached_keys.shape
    kv_heads = columns // HEAD_WIDTH
    query_heads = queries.reshape(requests, kv_heads, -1, HEAD_WIDTH)
    key_heads = cached_keys.reshape(requests, span_len, kv_heads, HEAD_WIDTH)
    value_heads = cached_values.reshape(requests, span_len, kv_heads, HEAD_WIDTH)
    own_key = new_keys.reshape(requests, kv_heads, HEAD_WIDTH)
    own_value = new_values.reshape(requests, kv_heads, HEAD_WIDTH)
    scaling = HEAD_WIDTH ** (-0.5)
    scores = (
        jnp.einsum("nhgd,nthd->nhgt", query_heads, key_heads, preferred_element_type=jnp.float32)
        * scaling
    )
    own_score = (
        jnp.einsum("nhgd,nhd->nhg", query_heads, own_key, preferred_element_type=jnp.float32)
        * scaling
    )
    live_mask = jnp.arange(span_len)[None, :] < lengths[:, None]
    scores = jnp.where(live_mask[:, None, None, :], scores, -1e30)
    row_top = jnp.maximum(jnp.max(scores, axis=-1), own_score)
    weights = jnp.exp(scores - row_top[..., None])
    own_weight = jnp.exp(own_score - row_top)
    totals = jnp.sum(weights, axis=-1) + own_weight
    shares = (weights / totals[..., None]).astype(jnp.bfloat16)
    own_share = (own_weight / totals).astype(jnp.bfloat16)
    blended = jnp.einsum("nhgt,nthd->nhgd", shares, value_heads, preferred_element_type=jnp.float32)
    blended = (
        blended
        + own_share.astype(jnp.float32)[..., None] * own_value.astype(jnp.float32)[:, :, None, :]
    )
    return blended.astype(jnp.bfloat16).reshape(requests, -1)


def head_sums(parts):
    return (
        lax.psum_scatter(parts[0], "tp", scatter_dimension=1, tiled=True),
        lax.psum_scatter(parts[1], "tp", scatter_dimension=1, tiled=True),
        lax.psum_scatter(parts[2], "tp", scatter_dimension=1, tiled=True),
        lax.psum_scatter(parts[3], "tp", scatter_dimension=1, tiled=True),
    )


def shards(
    normed_input_rows,
    key_projection_weight,
    value_projection_weight,
    adapter_down_factors,
    adapter_up_factors,
    request_owner_replica,
    request_adapter_slot,
    prefill_adapter_slot,
    prefill_first_row,
    context_length,
    request_page_table,
    queries,
    rotated_cache_keys,
    paged_cache_values,
):
    decodes = request_adapter_slot.shape[0]
    adapter_store = adapter_down_factors.shape[0]
    local_width = rotated_cache_keys.shape[2]
    decode_input_rows = normed_input_rows[:decodes]
    prefill_input_rows = normed_input_rows[decodes:]
    key_dec = jnp.dot(decode_input_rows, key_projection_weight, preferred_element_type=jnp.float32)
    value_dec = jnp.dot(
        decode_input_rows, value_projection_weight, preferred_element_type=jnp.float32
    )
    key_pre = jnp.dot(prefill_input_rows, key_projection_weight, preferred_element_type=jnp.float32)
    value_pre = jnp.dot(
        prefill_input_rows, value_projection_weight, preferred_element_type=jnp.float32
    )
    selected_slot = prefill_adapter_slot[0]
    down_selected = lax.dynamic_index_in_dim(adapter_down_factors, selected_slot, 0, keepdims=False)
    up_selected = lax.dynamic_index_in_dim(adapter_up_factors, selected_slot, 0, keepdims=False)
    reduced_prefill = jnp.dot(prefill_input_rows, down_selected, preferred_element_type=jnp.float32)
    key_dec, value_dec, key_pre, value_pre = head_sums((key_dec, value_dec, key_pre, value_pre))
    reduced_prefill = lax.psum(reduced_prefill, "tp")
    extra_terms = jnp.einsum(
        "qg,gcv->qcv", reduced_prefill, up_selected.astype(jnp.float32), precision=highest_precision
    )
    key_pre = key_pre + extra_terms[:, 0]
    value_pre = value_pre + extra_terms[:, 1]
    replicas = lax.axis_size("rep")
    capacity = max(2, 2 * decodes // replicas)
    owner_ids = request_owner_replica[:, 0]
    member = (owner_ids[:, None] == jnp.arange(replicas)[None, :]).astype(jnp.int32)
    ranking = jnp.sum((jnp.cumsum(member, axis=0) - member) * member, axis=1)
    target = owner_ids * capacity + ranking
    placing = (target[:, None] == jnp.arange(replicas * capacity)[None, :]).astype(jnp.bfloat16)
    send_rows = (
        jnp.einsum("ns,ni->si", placing, decode_input_rows, preferred_element_type=jnp.float32)
        .astype(jnp.bfloat16)
        .reshape(replicas, capacity, -1)
    )
    slot_codes = (request_adapter_slot + 1).astype(jnp.float32)
    send_slot = (
        (
            jnp.einsum(
                "ns,n->s", placing.astype(jnp.float32), slot_codes, precision=highest_precision
            )
            - 1.0
        )
        .astype(jnp.bfloat16)
        .reshape(replicas, capacity)
    )
    incoming_rows = lax.all_to_all(send_rows, "rep", split_axis=0, concat_axis=0, tiled=True)
    slot_in = lax.all_to_all(send_slot, "rep", split_axis=0, concat_axis=0, tiled=True)
    selected_mask = (
        slot_in.astype(jnp.int32)[..., None] == jnp.arange(adapter_store)[None, None, :]
    ).astype(jnp.float32)
    reduced_every_row = jnp.einsum(
        "vrw,xwf->vrxf", incoming_rows, adapter_down_factors, preferred_element_type=jnp.float32
    )
    low_rank = jnp.einsum(
        "sca,scaj->scj", selected_mask, reduced_every_row, precision=highest_precision
    )
    low_rank = lax.psum(low_rank, "tp")
    up_rows = jnp.einsum(
        "ybl,lvzp->ybvzp",
        selected_mask,
        adapter_up_factors.astype(jnp.float32),
        precision=highest_precision,
    )
    back_low = lax.all_to_all(low_rank, "rep", split_axis=0, concat_axis=0, tiled=True)
    back_up = lax.all_to_all(
        up_rows.astype(jnp.bfloat16), "rep", split_axis=0, concat_axis=0, tiled=True
    )
    result_rows = jnp.einsum(
        "scr,scrkd->sckd", back_low, back_up.astype(jnp.float32), precision=highest_precision
    )
    decode_correction = jnp.einsum(
        "ns,skd->nkd",
        placing.astype(jnp.float32),
        result_rows.reshape(replicas * capacity, 2, local_width),
        precision=highest_precision,
    )
    key_dec = key_dec + decode_correction[:, 0]
    value_dec = value_dec + decode_correction[:, 1]
    positions_pre = prefill_first_row[0] + jnp.arange(prefill_input_rows.shape[0], dtype=jnp.int32)
    keys_new = rotate_heads(key_dec, context_length).astype(jnp.bfloat16)
    values_new = value_dec.astype(jnp.bfloat16)
    keys_pre = rotate_heads(key_pre, positions_pre).astype(jnp.bfloat16)
    decode_kv = jnp.stack([keys_new, values_new], axis=1)
    prefill_kv = jnp.stack([keys_pre, value_pre.astype(jnp.bfloat16)], axis=1)
    cached_keys = rotated_cache_keys[request_page_table].reshape(decodes, -1, local_width)
    cached_values = paged_cache_values[request_page_table].reshape(decodes, -1, local_width)
    attended = attend(queries, keys_new, values_new, cached_keys, cached_values, context_length)
    return (decode_kv, prefill_kv, attended)


def solution(mesh):
    in_specs = (
        P("rep", "tp"),
        P("tp", None),
        P("tp", None),
        P("rep", "tp", None),
        P("rep", None, None, "tp"),
        P("rep", None),
        P("rep"),
        P("rep"),
        P("rep"),
        P("rep"),
        P("rep", None),
        P("rep", "tp"),
        P("rep", None, "tp"),
        P("rep", None, "tp"),
    )
    out_specs = (P("rep", None, "tp"), P("rep", None, "tp"), P("rep", "tp"))
    return jax.shard_map(shards, mesh=mesh, in_specs=in_specs, out_specs=out_specs, check_vma=False)
```

profile of v0, /device:TPU:1, one launch (start us, length us, event | category | flops | bytes accessed | tf_op | source)
XLA Modules:
  0.0 222.9 jit_solution(6426592215430735210)
XLA Ops:
  11.3 13.0 %all-to-all-start = ((bf16[64,1,2]{2,1,0:T(2,128)(2,1)}), bf16[64,1,2]{2,1,0:T(2,128)(2,1)S(1)}, u32[]{:S(2)}, u32[]{:S(2)}) async-start(bf16[64,1,2]{2,1,0:T(2,128)(2,1)} %all_to_all.20), calls=%async_computation.1 | async-start | bytes 65536 | tf_op jit(solution)/shard_map/all_to_all | solution.py:140
  25.0 4.2 %fusion.8 = f32[960,64]{0,1:T(8,128)} fusion(bf16[1024,2048]{1,0:T(8,128)(2,1)} %param.14, bf16[4,2048,64]{1,2,0:T(8,128)(2,1)} %param.17, s32[]{:T(128)S(6)} %select_n.18), kind=kOutput, calls=%fused_computation.12 | convolution fusion | flops 251658240 | bytes 4440068 | tf_op jit(solution)/shard_map/dot_general | solution.py:108
  29.3 6.5 %fusion.2 = f32[960,512]{0,1:T(8,128)} fusion(bf16[2048,512]{1,0:T(8,128)(2,1)} %param.16, bf16[1024,2048]{1,0:T(8,128)(2,1)} %param.14), kind=kOutput, calls=%fused_computation.4 | convolution fusion | flops 2013265920 | bytes 7995392 | tf_op jit(solution)/shard_map/dot_general | solution.py:102
  35.8 1.4 convolution_convert_fusion.1
  38.4 10.3 %all-to-all-start.1 = ((bf16[64,2,2048]{2,1,0:T(2,128)(2,1)}), bf16[64,2,2048]{2,1,0:T(2,128)(2,1)S(1)}, u32[]{:S(2)}, u32[]{:S(2)}) async-start(bf16[64,2,2048]{2,1,0:T(2,128)(2,1)} %reshape.335), calls=%async_computation.2 | async-start | bytes 1048576 | tf_op jit(solution)/shard_map/all_to_all | solution.py:139
  49.0 17.4 %all-to-all-done.1 = bf16[64,2,2048]{2,1,0:T(2,128)(2,1)S(1)} async-done(((bf16[64,2,2048]{2,1,0:T(2,128)(2,1)}), bf16[64,2,2048]{2,1,0:T(2,128)(2,1)S(1)}, u32[]{:S(2)}, u32[]{:S(2)}) %all-to-all-start.1) | async-done | bytes 524320 | tf_op jit(solution)/shard_map/all_to_all | solution.py:139
  66.4 1.9 fusion.16
  69.0 14.1 %psum.14 = f32[64,2,64]{2,1,0:T(2,128)S(1)} all-reduce(f32[64,2,64]{2,1,0:T(2,128)S(1)} %bitcast.136), channel_id=1, replica_groups=mesh['rep'=64,'tp'=4] {'tp'}, use_global_device_ids=true, to_apply=%region_3.4 | all-reduce | flops 8192 | bytes 65536 | tf_op jit(solution)/shard_map/psum | solution.py:150
  83.9 9.4 %all-to-all-start.2 = ((f32[64,1,128]{2,1,0:T(1,128)}), f32[64,1,128]{2,1,0:T(1,128)S(1)}, u32[]{:S(2)}, u32[]{:S(2)}) async-start(f32[64,1,128]{2,1,0:T(1,128)} %reshape.380), calls=%async_computation.3 | async-start | bytes 65536 | tf_op jit(solution)/shard_map/all_to_all | solution.py:157
  94.7 6.3 %copy.49 = bf16[64,2,64,2,128]{4,3,2,1,0:T(2,128)(2,1)} copy(bf16[64,2,64,2,128]{4,0,3,2,1:T(8,128)(2,1)S(1)} %convolution_convert_fusion) | data formatting | bytes 8388608 | tf_op jit(solution)/shard_map/convert_element_type | solution.py:159
  101.0 1.7 all-to-all-done.2
  103.3 8.8 %all-to-all-start.3 = ((bf16[64,2,64,2,128]{4,3,2,1,0:T(2,128)(2,1)}), bf16[64,2,64,2,128]{4,3,2,1,0:T(2,128)(2,1)}, u32[]{:S(2)}, u32[]{:S(2)}) async-start(bf16[64,2,64,2,128]{4,3,2,1,0:T(2,128)(2,1)} %copy.49), calls=%async_computation.4 | async-start | bytes 8388608 | tf_op jit(solution)/shard_map/all_to_all | solution.py:158
  112.1 5.8 %fusion.6 = f32[960,512]{0,1:T(8,128)} fusion(bf16[2048,512]{1,0:T(8,128)(2,1)S(1)} %copy-done, bf16[1024,2048]{1,0:T(8,128)(2,1)} %param.14), kind=kOutput, calls=%fused_computation.8 | convolution fusion | flops 2013265920 | bytes 7995392 | tf_op jit(solution)/shard_map/dot_general | solution.py:101
  118.1 2.1 fusion.42
  120.4 2.8 %fusion.39 = f32[64,512]{1,0:T(8,128)} fusion(bf16[2048,512]{1,0:T(8,128)(2,1)} %param.16, bf16[1024,2048]{1,0:T(8,128)(2,1)} %param.14), kind=kOutput, calls=%fused_computation.51 | convolution fusion | flops 134217728 | bytes 2490368 | tf_op jit(solution)/shard_map/dot_general | solution.py:98
  123.6 2.1 gather_fusion
  125.7 3.0 %gather_fusion.1 = bf16[256,16,128]{2,1,0:T(8,128)(2,1)} fusion(bf16[256,16,128]{2,1,0:T(8,128)(2,1)} %param.27, s32[1024]{0:T(1024)S(1)} %pad_clamp_fusion), kind=kCustom, calls=%fused_computation.1 | custom fusion | bytes 2098176 | tf_op jit(solution)/shard_map/gather | solution.py:179
  130.1 1.3 fusion.84
  131.5 1.6 fusion.32
  133.6 2.1 reduce.4
  135.7 1.5 reshape.381
  137.2 12.6 %reduce-scatter.9.cloned.1.call-done = f32[960,128]{0,1:T(8,128)} async-done(((f32[960,512]{0,1:T(8,128)}), f32[960,128]{0,1:T(8,128)}) %reduce-scatter.9.cloned.1.call-update) | async-done | bytes 491536 | tf_op jit(solution)/shard_map/reduce_scatter | solution.py:71
  153.5 53.0 %all-to-all-done.3 = bf16[64,2,64,2,128]{4,3,2,1,0:T(2,128)(2,1)} async-done(((bf16[64,2,64,2,128]{4,3,2,1,0:T(2,128)(2,1)}), bf16[64,2,64,2,128]{4,3,2,1,0:T(2,128)(2,1)}, u32[]{:S(2)}, u32[]{:S(2)}) %all-to-all-start.3) | async-done | bytes 4194336 | tf_op jit(solution)/shard_map/all_to_all | solution.py:158
  206.5 4.0 %fusion = f32[64,2,1,2,128]{4,2,3,1,0:T(1,128)S(1)} fusion(f32[64,2,64,1,1]{2,3,4,1,0:T(1,128)} %bitcast.128, bf16[64,2,64,2,128]{4,3,2,1,0:T(2,128)(2,1)} %all-to-all-done.3), kind=kOutput, calls=%fused_computation.2 | convolution fusion | flops 25165824 | bytes 4358144 | tf_op jit(solution)/shard_map/scr,scrkd->sckd/dot_general | solution.py:161
  (71 shorter events, 20.5 us)
Async XLA Ops:
  7.2 105.0 %copy-start = (bf16[2048,512]{1,0:T(8,128)(2,1)S(1)}, bf16[2048,512]{1,0:T(8,128)(2,1)}, u32[]{:S(2)}) copy-start(bf16[2048,512]{1,0:T(8,128)(2,1)} %param.15) | copy-start | bytes 6291460
  11.3 27.1 %all-to-all-start = ((bf16[64,1,2]{2,1,0:T(2,128)(2,1)}), bf16[64,1,2]{2,1,0:T(2,128)(2,1)S(1)}, u32[]{:S(2)}, u32[]{:S(2)}) async-start(bf16[64,1,2]{2,1,0:T(2,128)(2,1)} %all_to_all.20), calls=%async_computation.1 | async-start | bytes 65536 | tf_op jit(solution)/shard_map/all_to_all | solution.py:140
  24.3 107.1 %all-reduce.2.cloned.1.call-start = ((), (), s32[]{:S(2)}) async-start(), calls=%async_computation.11 | async-start | bytes 524288 | tf_op jit(solution)/shard_map/psum | solution.py:110
  29.2 108.0 %reduce-scatter.11.cloned.1.call-start = ((), (), s32[]{:S(2)}) async-start(), calls=%async_computation.12 | async-start | bytes 2621440 | tf_op jit(solution)/shard_map/reduce_scatter | solution.py:72
  35.8 57.6 %copy-start.2 = (bf16[4,64,2,128]{3,2,1,0:T(2,128)(2,1)S(1)}, bf16[4,64,2,128]{3,2,1,0:T(2,128)(2,1)}, u32[]{:S(2)}) copy-start(bf16[4,64,2,128]{3,2,1,0:T(2,128)(2,1)} %param.18) | copy-start | bytes 393220
  38.4 28.0 %all-to-all-start.1 = ((bf16[64,2,2048]{2,1,0:T(2,128)(2,1)}), bf16[64,2,2048]{2,1,0:T(2,128)(2,1)S(1)}, u32[]{:S(2)}, u32[]{:S(2)}) async-start(bf16[64,2,2048]{2,1,0:T(2,128)(2,1)} %reshape.335), calls=%async_computation.2 | async-start | bytes 1048576 | tf_op jit(solution)/shard_map/all_to_all | solution.py:139
  83.9 18.8 %all-to-all-start.2 = ((f32[64,1,128]{2,1,0:T(1,128)}), f32[64,1,128]{2,1,0:T(1,128)S(1)}, u32[]{:S(2)}, u32[]{:S(2)}) async-start(f32[64,1,128]{2,1,0:T(1,128)} %reshape.380), calls=%async_computation.3 | async-start | bytes 65536 | tf_op jit(solution)/shard_map/all_to_all | solution.py:157
  102.7 0.6 copy-start.4
  103.3 103.2 %all-to-all-start.3 = ((bf16[64,2,64,2,128]{4,3,2,1,0:T(2,128)(2,1)}), bf16[64,2,64,2,128]{4,3,2,1,0:T(2,128)(2,1)}, u32[]{:S(2)}, u32[]{:S(2)}) async-start(bf16[64,2,64,2,128]{4,3,2,1,0:T(2,128)(2,1)} %copy.49), calls=%async_computation.4 | async-start | bytes 8388608 | tf_op jit(solution)/shard_map/all_to_all | solution.py:158
  112.1 37.8 %reduce-scatter.9.cloned.1.call-start = ((), (), s32[]{:S(2)}) async-start(), calls=%async_computation.10 | async-start | bytes 2621440 | tf_op jit(solution)/shard_map/reduce_scatter | solution.py:71
  118.0 5.3 %copy-start.6 = (s32[64]{0:T(128)S(1)}, s32[64]{0:T(128)}, u32[]{:S(2)}) copy-start(s32[64]{0:T(128)} %param.23) | copy-start | bytes 772
  118.0 5.3 %copy-start.3 = (bf16[64,1024]{1,0:T(8,128)(2,1)S(1)}, bf16[64,1024]{1,0:T(8,128)(2,1)}, u32[]{:S(2)}) copy-start(bf16[64,1024]{1,0:T(8,128)(2,1)} %param.25) | copy-start | bytes 393220
  118.0 5.4 %copy-start.5 = (s32[64,4]{0,1:T(4,128)S(1)}, s32[64,4]{0,1:T(4,128)}, u32[]{:S(2)}) copy-start(s32[64,4]{0,1:T(4,128)} %param.24) | copy-start | bytes 3076
  118.0 93.4 %reduce-scatter.5.cloned.1.call-start = ((), (), s32[]{:S(2)}) async-start(), calls=%async_computation.8 | async-start | bytes 163840 | tf_op jit(solution)/shard_map/reduce_scatter | solution.py:69
  120.2 91.2 %reduce-scatter.7.cloned.1.call-start = ((), (), s32[]{:S(2)}) async-start(), calls=%async_computation.9 | async-start | bytes 163840 | tf_op jit(solution)/shard_map/reduce_scatter | solution.py:70
  153.5 61.0 %copy-start.1 = (bf16[256,16,128]{2,1,0:T(8,128)(2,1)S(1)}, bf16[256,16,128]{2,1,0:T(8,128)(2,1)}, u32[]{:S(2)}) copy-start(bf16[256,16,128]{2,1,0:T(8,128)(2,1)} %gather_fusion.1) | copy-start | bytes 3145732
Sparse Core Ops, SparseCore 0:
  29.3 45.8 all-reduce.1
  78.0 34.8 reduce-scatter.10
  118.1 31.6 reduce-scatter.8
  152.4 21.2 reduce-scatter.4
  176.6 22.3 reduce-scatter.6
where the time goes:
time: 225 us; the launch traced here: 223 us
  waiting for transfers between devices  84.8 us (38%)
  starting transfers between devices  42 us (19%)
  matrix products  36 us (16%)
  local copies, waits for them, and re-layouts  20.4 us (9%)
  between operations  15.4 us (7%)
  blocking collectives  14.1 us (6%)
  other arithmetic  10.2 us (5%)
    all_to_all x1, waiting for transfers between devices, shards(): lax.all_to_all(up_rows.astype(jnp.bfloat16), 'rep', split_axis=0, concat_...  53 us
    all_to_all x1, waiting for transfers between devices, shards(): lax.all_to_all(send_rows, 'rep', split_axis=0, concat_axis=0, tiled=True)  17.4 us
    psum x1, blocking collectives, shards(): low_rank = lax.psum(low_rank, 'tp')  14.1 us
    all_to_all x1, starting transfers between devices, shards(): lax.all_to_all(send_slot, 'rep', split_axis=0, concat_axis=0, tiled=True)  13 us
    reduce_scatter x1, waiting for transfers between devices, head_sums(): lax.psum_scatter(parts[2], 'tp', scatter_dimension=1, tiled=True)  12.6 us
    all_to_all x1, starting transfers between devices, shards(): lax.all_to_all(send_rows, 'rep', split_axis=0, concat_axis=0, tiled=True)  10.3 us
    all_to_all x1, starting transfers between devices, shards(): lax.all_to_all(low_rank, 'rep', split_axis=0, concat_axis=0, tiled=True)  9.45 us
    all_to_all x1, starting transfers between devices, shards(): lax.all_to_all(up_rows.astype(jnp.bfloat16), 'rep', split_axis=0, concat_...  8.8 us
  transfers between devices with their start and end apart: 9, of which 4 were waited for; matrix products, arithmetic and copies ran while one was open for 26% of the time, Pallas kernels for 0%

commit v1 on v0

v1 whole, which is shorter than its diff:
```python
import jax
import jax.numpy as jnp
import numpy as np
from jax import lax
from jax.experimental import pallas as pl
from jax.experimental.pallas import tpu as pltpu
from jax.sharding import PartitionSpec as P

HEAD = 128
HALF = HEAD // 2
ROPE_BASE = 500000.0
PLANE = 8
BLOCKS = 4
CHUNKS = 2
GROUP = 16
PIECE = 64
MESH = pl.DeviceIdType.MESH
F32 = jnp.float32
BF16 = jnp.bfloat16


def mm(a, b):
    return lax.dot_general(a, b, (((1,), (0,)), ((), ())), preferred_element_type=F32)


def mt(a, b):
    return lax.dot_general(a, b, (((1,), (1,)), ((), ())), preferred_element_type=F32)


def iota(shape, axis):
    return lax.broadcasted_iota(jnp.int32, shape, axis)


def one_hot(condition):
    return jnp.where(condition, 1.0, 0.0).astype(BF16)


def trig(step, count):
    frequency = ROPE_BASE ** (-2.0 * np.arange(HALF) / HEAD)
    angles = step * np.arange(count)[:, None] * np.tile(frequency, 2)[None, :]
    return np.concatenate([np.cos(angles), np.sin(angles)], axis=1).astype(np.float32)


def kernel(
    x_hbm,
    wk_hbm,
    wv_hbm,
    d_hbm,
    up_ref,
    owner_ref,
    slot_ref,
    pslot_ref,
    pfirst_ref,
    length_ref,
    table_ref,
    q_hbm,
    kpool_hbm,
    vpool_hbm,
    low_ref,
    high_ref,
    dec_out,
    pre_out,
    att_out,
    x,
    w,
    d,
    q,
    kpool,
    vpool,
    kbuf,
    vbuf,
    s1a,
    s1b,
    r1a,
    r1b,
    s2a,
    s2b,
    r2a,
    r2b,
    s3,
    r3,
    s4,
    r4,
    uall,
    ug,
    ysend,
    yrecv,
    sr,
    sd,
    sc,
    rr,
    rd,
    rc,
    lrp,
    own,
    stage,
    dec,
    base,
    lens,
    m_s,
    l_s,
    o_s,
    load_sem,
    z1s,
    z1r,
    p1s,
    p1r,
    us,
    ur,
    ys,
    yr,
    ns,
    nr,
    p2s,
    p2r,
    z2s,
    z2r,
):
    t = lax.axis_index("tp")
    rep = lax.axis_index("rep")
    tps = lax.axis_size("tp")
    planes = lax.axis_size("rep") // PLANE
    z = lax.div(rep, PLANE)
    p = lax.rem(rep, PLANE)
    rows = x.shape[0] // BLOCKS
    decodes = q.shape[0]
    slots = 2 * lax.axis_size("rep")
    width = x.shape[1] // CHUNKS
    s1, r1, s2, r2 = (s1a, s1b), (r1a, r1b), (s2a, s2b), (r2a, r2b)

    barrier = pltpu.get_barrier_semaphore()

    def at(rep_to, tp_to):
        return dict(device_id=(rep_to, tp_to), device_id_type=MESH)

    def z_of(dd):
        return lax.rem(z + dd, planes)

    def p_of(dd):
        return lax.rem(p + dd, PLANE)

    def t_of(dd):
        return lax.rem(t + dd, tps)

    def each(low, high, body):
        lax.fori_loop(low, high, lambda i, c: (body(i), c)[1], 0)

    each(1, planes, lambda k: pl.semaphore_signal(barrier, inc=1, **at(z_of(k) * PLANE + p, t)))
    each(1, PLANE, lambda k: pl.semaphore_signal(barrier, inc=1, **at(z * PLANE + p_of(k), t)))
    each(1, tps, lambda k: pl.semaphore_signal(barrier, inc=1, **at(rep, t_of(k))))

    def load(source, target, k):
        return pltpu.make_async_copy(source, target, load_sem.at[k])

    def x_load(b):
        part = pl.ds(b * rows, rows)
        return load(x_hbm.at[part], x.at[part], b)

    def w_load(j):
        columns = pl.ds(pl.multiple_of(t_of(j) * HEAD, HEAD), HEAD)
        return (
            load(wk_hbm.at[:, columns], w.at[j, :, pl.ds(0, HEAD)], BLOCKS + 2 * j),
            load(wv_hbm.at[:, columns], w.at[j, :, pl.ds(HEAD, HEAD)], BLOCKS + 2 * j + 1),
        )

    k0 = BLOCKS + 2 * 4
    q_load = load(q_hbm, q, k0)
    d_load = load(d_hbm, d, k0 + 1)
    kpool_load = load(kpool_hbm, kpool, k0 + 2)
    vpool_load = load(vpool_hbm, vpool, k0 + 3)
    x_load(0).start()
    d_load.start()
    for c in w_load(2):
        c.start()
    for b in (1, 2, 3):
        x_load(b).start()
    for j in (3, 1, 0):
        for c in w_load(j):
            c.start()
    for c in (q_load, kpool_load, vpool_load):
        c.start()

    eye = iota((decodes, decodes), 0) == iota((decodes, decodes), 1)

    def column(row):
        return jnp.sum(jnp.where(eye, jnp.broadcast_to(row, eye.shape), 0.0), axis=1, keepdims=True)

    owner_row = owner_ref[...].astype(F32)
    owner_col = column(owner_row)
    same = owner_col == owner_row
    before_col = iota(eye.shape, 1) < iota(eye.shape, 0)
    before_row = iota(eye.shape, 0) < iota(eye.shape, 1)
    target_col = 2.0 * owner_col + jnp.sum(
        jnp.where(same & before_col, 1.0, 0.0), axis=1, keepdims=True
    )
    target_row = 2.0 * owner_row + jnp.sum(
        jnp.where(same & before_row, 1.0, 0.0), axis=0, keepdims=True
    )
    placing = one_hot(target_row == iota((slots, decodes), 0).astype(F32))
    placing_back = one_hot(target_col == iota((decodes, slots), 1).astype(F32))
    codes = jnp.broadcast_to(column(slot_ref[...].astype(F32)) + 1.0, (decodes, HEAD)).astype(BF16)
    lens[...] = jnp.broadcast_to(column(length_ref[...].astype(F32)), (decodes, HEAD))

    x_load(0).wait()
    for c in range(CHUNKS):
        placed = mm(placing, x[0:decodes, c * width : (c + 1) * width]).astype(BF16)
        s1[c][:, :, 0:width] = placed.reshape(planes, 16, width)
    s1a[:, :, width : width + HEAD] = mm(placing, codes).astype(BF16).reshape(planes, 16, HEAD)

    pairs = up_ref[...]
    count = pairs.shape[0] // 2
    pick = iota((count, 2 * count), 1) - 2 * iota((count, 2 * count), 0)
    rank = uall.shape[1]
    uall[:, :, 0:HEAD] = mm(one_hot(pick == 0), pairs).astype(BF16).reshape(-1, rank, HEAD)
    uall[:, :, HEAD:] = mm(one_hot(pick == 1), pairs).astype(BF16).reshape(-1, rank, HEAD)
    selected = pslot_ref[0]
    ug[t] = uall[selected]

    def z1_copy(c, k):
        to = z_of(k)
        return pltpu.make_async_remote_copy(
            s1[c].at[to], r1[c].at[z], z1s.at[c, k], z1r.at[c, k], **at(to * PLANE + p, t)
        )

    def p1_copy(c, k):
        to = p_of(k)
        return pltpu.make_async_remote_copy(
            s2[c].at[to], r2[c].at[p], p1s.at[c, k], p1r.at[c, k], **at(z * PLANE + to, t)
        )

    def p2_copy(k):
        to = p_of(k)
        return pltpu.make_async_remote_copy(
            s3.at[to], r3.at[p], p2s.at[k], p2r.at[k], **at(z * PLANE + to, t)
        )

    def z2_copy(k):
        to = z_of(k)
        return pltpu.make_async_remote_copy(
            s4.at[to], r4.at[z], z2s.at[k], z2r.at[k], **at(to * PLANE + p, t)
        )

    def up_copy(k):
        return pltpu.make_async_remote_copy(
            ug.at[t], ug.at[t], us.at[k], ur.at[k], **at(rep, t_of(k))
        )

    def low_copy(k):
        return pltpu.make_async_remote_copy(
            ysend, yrecv.at[k - 1], ns.at[k], nr.at[k], **at(rep, t_of(k))
        )

    def ahead(b):
        return 1 + 2 * lax.div(b, 2)

    def back(b):
        return 3 - 2 * lax.div(b, 2)

    def relay_copy(b):
        return pltpu.make_async_remote_copy(
            sr.at[b], rr.at[b], ys.at[0, b], yr.at[0, b], **at(rep, t_of(ahead(b)))
        )

    def direct_copy(b):
        return pltpu.make_async_remote_copy(
            sd.at[b], rd.at[b], ys.at[1, b], yr.at[1, b], **at(rep, t_of(back(b)))
        )

    def sum_copy(b):
        return pltpu.make_async_remote_copy(
            sc.at[b], rc.at[b], ys.at[2, b], yr.at[2, b], **at(rep, t_of(ahead(b)))
        )

    pl.semaphore_wait(barrier, planes - 1 + PLANE - 1 + tps - 1)
    each(1, tps, lambda k: up_copy(k).start())
    for c in range(CHUNKS):
        each(1, planes, lambda k: z1_copy(c, k).start())
    for c in range(CHUNKS):
        r1[c][z] = s1[c][z]

    first = pfirst_ref[0]
    high = high_ref[pl.ds(lax.div(first, PIECE), 1), :]
    low = low_ref[pl.ds(lax.rem(first, PIECE), 1), :]

    def turn(a, b):
        ca, sa, cb, sb = a[:, 0:HEAD], a[:, HEAD:], b[:, 0:HEAD], b[:, HEAD:]
        return ca * cb - sa * sb, sa * cb + ca * sb

    c0, s0 = turn(high, low)
    steps = high_ref[0:16, :]
    cb, sb = steps[:, 0:HEAD], steps[:, HEAD:]
    base[:, 0:HEAD] = c0 * cb - s0 * sb
    base[:, HEAD:] = s0 * cb + c0 * sb

    swap_out = iota((slots, slots), 0)
    swap_in = iota((slots, slots), 1)
    swap = one_hot(
        swap_in == ((swap_out >> 1) & 7) * 16 + (swap_out >> 4) * 2 + (swap_out & 1)
    )

    d_load.wait()
    for c in w_load(2):
        c.wait()
    each(1, tps, lambda k: up_copy(k).wait_recv())

    def part_of(b, j):
        here = pl.ds(pl.multiple_of(b * rows, rows), rows)
        return mm(x[here, :], w[j]) + mm(lrp[here, :], ug[t_of(j)])

    def relay_step(b):
        here = pl.ds(pl.multiple_of(b * rows, rows), rows)

        @pl.when(b > 0)
        def _():
            x_load(b).wait()

        low_rank = mt(x[here, :], d[selected])
        row = iota(low_rank.shape, 0) + b * rows
        lrp[here, :] = jnp.where(row >= decodes, low_rank, 0.0).astype(BF16)
        sr[b] = part_of(b, 2).astype(BF16)
        relay_copy(b).start()

    def direct_step(b):
        sd[b] = part_of(b, back(b)).astype(BF16)
        direct_copy(b).start()

    def sum_step(b):
        part = part_of(b, ahead(b))
        relay_copy(b).wait_recv()
        sc[b] = (part + rr[b].astype(F32)).astype(BF16)
        sum_copy(b).start()

    def own_step(b):
        own[pl.ds(pl.multiple_of(b * rows, rows), rows), :] = part_of(b, 0)

    def order(i):
        return lax.div(i, 2) + 2 * lax.rem(i, 2)

    each(0, BLOCKS, lambda i: relay_step(order(i)))
    for j in (3, 1):
        for c in w_load(j):
            c.wait()
    each(0, BLOCKS, lambda i: direct_step(order(i)))
    each(0, BLOCKS, lambda i: sum_step(order(i)))

    def forward(c):
        each(1, planes, lambda k: z1_copy(c, k).wait_recv())
        moved = mm(swap, r1[c][...].reshape(slots, -1)).astype(BF16)
        s2[c][...] = moved.reshape(PLANE, 16, -1)
        each(1, PLANE, lambda k: p1_copy(c, k).start())
        r2[c][p] = s2[c][p]

    forward(0)
    for c in w_load(0):
        c.wait()
    each(0, BLOCKS, own_step)

    for c in (q_load, kpool_load, vpool_load):
        c.wait()
    maxp, page = table_ref.shape[0], kpool.shape[1]
    span = maxp * page

    def gather(i):
        for j in range(maxp):
            number = table_ref[j, i]
            here = pl.ds(pl.multiple_of((i * maxp + j) * page, page), page)
            kbuf[here, :] = kpool[number]
            vbuf[here, :] = vpool[number]

    each(0, decodes, gather)
    heads = q.shape[1] // HEAD
    scale = HEAD**-0.5

    def queries_of(i):
        here = pl.ds(pl.multiple_of(i * GROUP, GROUP), GROUP)
        return jnp.concatenate(
            [q[here, g * HEAD : (g + 1) * HEAD] for g in range(heads)], axis=0
        )

    def cached(i):
        here = pl.ds(pl.multiple_of(i * GROUP * span, GROUP * span), GROUP * span)
        scores = mt(queries_of(i), kbuf[here, :]) * scale
        length = lens[pl.ds(pl.multiple_of(i * GROUP, GROUP), GROUP), 0:1]
        length = jnp.concatenate([length] * heads, axis=0)
        begin = (iota(length.shape, 0) & (GROUP - 1)) * span
        end = begin + length.astype(jnp.int32)
        place = iota(scores.shape, 1)
        scores = jnp.where((place >= begin) & (place < end), scores, -1e30)
        top = jnp.max(scores, axis=1, keepdims=True)
        weights = jnp.exp(scores - top)
        o_s[i] = mm(weights.astype(BF16), vbuf[here, :])
        m_s[i] = jnp.broadcast_to(top, (GROUP * heads, HEAD))
        l_s[i] = jnp.broadcast_to(jnp.sum(weights, axis=1, keepdims=True), (GROUP * heads, HEAD))

    each(0, decodes // GROUP, cached)
    forward(1)

    partial = jnp.zeros((slots, d.shape[0] * rank), F32)
    for c in range(CHUNKS):
        each(1, PLANE, lambda k: p1_copy(c, k).wait_recv())
        factors = d[:, :, c * width : (c + 1) * width].reshape(-1, width)
        partial = partial + mt(r2[c][:, :, 0:width].reshape(slots, width), factors)
    code = r2a[:, :, width : width + HEAD].reshape(slots, HEAD).astype(F32)
    lane_slot = (iota((slots, HEAD), 1) >> 6) + 1
    lane_slot = lane_slot.astype(F32)
    low_half = code == lane_slot
    high_half = code == lane_slot + 2.0
    mine = jnp.where(low_half, partial[:, 0:HEAD], 0.0) + jnp.where(
        high_half, partial[:, HEAD:], 0.0
    )
    ysend[...] = mine.astype(BF16)
    each(1, tps, lambda k: low_copy(k).start())

    sign = jnp.where(iota((1, HEAD), 1) < HALF, -1.0, 1.0)

    def rotated(keys, cosine, sine):
        return keys * cosine + pltpu.roll(keys, HALF, 1) * (sine * sign)

    def finish(b):
        here = pl.ds(pl.multiple_of(b * rows, rows), rows)
        direct_copy(b).wait_recv()
        sum_copy(b).wait_recv()
        total = own[here, :] + rd[b].astype(F32) + rc[b].astype(F32)
        own[here, :] = total
        low_c, low_s = low_ref[0:PIECE, 0:HEAD], low_ref[0:PIECE, HEAD:]
        for i in range(rows // PIECE):
            if b == 0 and i == 0:
                continue
            a = b * (rows // PIECE) + i - 1
            ca, sa = base[a : a + 1, 0:HEAD], base[a : a + 1, HEAD:]
            piece = total[i * PIECE : (i + 1) * PIECE]
            keys = rotated(piece[:, 0:HEAD], ca * low_c - sa * low_s, sa * low_c + ca * low_s)
            stage[pl.ds(2 * i * PIECE, PIECE, stride=2), :] = keys
            stage[pl.ds(2 * i * PIECE + 1, PIECE, stride=2), :] = piece[:, HEAD:]
        skip = 2 * PIECE if b == 0 else 0
        begin = 2 * (b * rows - decodes) + skip
        pre_out[begin : begin + 2 * rows - skip, :] = stage[skip:, :].astype(BF16)

    finish(0)
    finish(2)

    each(1, tps, lambda k: low_copy(k).wait_recv())
    whole = mine
    for k in range(3):
        whole = whole + yrecv[k].astype(F32)
    wide = jnp.concatenate(
        [jnp.where(low_half, whole, 0.0), jnp.where(high_half, whole, 0.0)], axis=1
    )
    coarse = wide.astype(BF16)
    fine = (wide - coarse.astype(F32)).astype(BF16)
    factors = uall[...].reshape(-1, 2 * HEAD)
    delta = mm(coarse, factors) + mm(fine, factors)
    s3[...] = delta.astype(BF16).reshape(PLANE, 16, 2 * HEAD)
    each(1, PLANE, lambda k: p2_copy(k).start())
    r3[p] = s3[p]

    finish(1)

    each(1, PLANE, lambda k: p2_copy(k).wait_recv())
    s4[...] = mm(swap, r3[...].reshape(slots, -1)).astype(BF16).reshape(planes, 16, -1)
    each(1, planes, lambda k: z2_copy(k).start())
    r4[z] = s4[z]

    finish(3)

    chosen = lens[:, 0:1] == iota((decodes, low_ref.shape[0]), 1).astype(F32)
    angles = lax.dot_general(
        jnp.where(chosen, 1.0, 0.0),
        low_ref[...],
        (((1,), (0,)), ((), ())),
        precision=lax.Precision.HIGHEST,
        preferred_element_type=F32,
    )
    each(1, planes, lambda k: z2_copy(k).wait_recv())
    both = own[0:decodes, :] + mm(placing_back, r4[...].reshape(slots, -1))
    keys = rotated(both[:, 0:HEAD], angles[:, 0:HEAD], angles[:, HEAD:]).astype(BF16).astype(F32)
    values = both[:, HEAD:].astype(BF16).astype(F32)
    dec[pl.ds(0, decodes, stride=2), :] = keys
    dec[pl.ds(1, decodes, stride=2), :] = values
    dec_out[...] = dec[...].astype(BF16)
    for i in range(decodes // GROUP):
        key = jnp.concatenate([keys[i * GROUP : (i + 1) * GROUP]] * heads, axis=0)
        value = jnp.concatenate([values[i * GROUP : (i + 1) * GROUP]] * heads, axis=0)
        score = jnp.sum(queries_of(i).astype(F32) * key, axis=1, keepdims=True) * scale
        old = m_s[i]
        top = jnp.maximum(old, score)
        shrink = jnp.exp(old - top)
        share = jnp.exp(score - top)
        result = (o_s[i] * shrink + share * value) / (l_s[i] * shrink + share)
        for g in range(heads):
            att_out[i * GROUP : (i + 1) * GROUP, g * HEAD : (g + 1) * HEAD] = result[
                g * GROUP : (g + 1) * GROUP
            ].astype(BF16)

    for c in range(CHUNKS):
        each(1, planes, lambda k: z1_copy(c, k).wait_send())
        each(1, PLANE, lambda k: p1_copy(c, k).wait_send())
    each(1, planes, lambda k: z2_copy(k).wait_send())
    each(1, PLANE, lambda k: p2_copy(k).wait_send())
    each(1, tps, lambda k: up_copy(k).wait_send())
    each(1, tps, lambda k: low_copy(k).wait_send())

    def sent(b):
        relay_copy(b).wait_send()
        direct_copy(b).wait_send()
        sum_copy(b).wait_send()

    each(0, BLOCKS, sent)


def shards(
    normed_input_rows,
    key_projection_weight,
    value_projection_weight,
    adapter_down_factors,
    adapter_up_factors,
    request_owner_replica,
    request_adapter_slot,
    prefill_adapter_slot,
    prefill_first_row,
    context_length,
    request_page_table,
    queries,
    rotated_cache_keys,
    paged_cache_values,
):
    total, width = normed_input_rows.shape
    decodes = request_adapter_slot.shape[0]
    adapters, _, rank = adapter_down_factors.shape
    pages, page, local = rotated_cache_keys.shape
    slots = 2 * lax.axis_size("rep")
    planes = lax.axis_size("rep") // PLANE
    tps = lax.axis_size("tp")
    rows = total // BLOCKS
    part = width // CHUNKS
    prefills = total - decodes
    groups = decodes // GROUP
    heads = queries.shape[1] // HEAD
    span = decodes * request_page_table.shape[1] * page
    vmem = pl.BlockSpec(memory_space=pltpu.VMEM)
    smem = pl.BlockSpec(memory_space=pltpu.SMEM)
    hbm = pl.BlockSpec(memory_space=pl.ANY)
    dma = pltpu.SemaphoreType.DMA

    def bf(*shape):
        return pltpu.VMEM(shape, BF16)

    def fl(*shape):
        return pltpu.VMEM(shape, F32)

    decode_kv, prefill_kv, attended = pl.pallas_call(
        kernel,
        out_shape=(
            jax.ShapeDtypeStruct((2 * decodes, HEAD), BF16),
            jax.ShapeDtypeStruct((2 * prefills, HEAD), BF16),
            jax.ShapeDtypeStruct(queries.shape, BF16),
        ),
        in_specs=[hbm, hbm, hbm, hbm, vmem, vmem, vmem, smem, smem, vmem, smem, hbm, hbm, hbm, vmem, vmem],
        out_specs=(vmem, vmem, vmem),
        scratch_shapes=[
            bf(total, width),
            bf(tps, width, 2 * HEAD),
            bf(adapters, rank, width),
            bf(*queries.shape),
            bf(pages, page, local),
            bf(pages, page, local),
            bf(span, HEAD),
            bf(span, HEAD),
            bf(planes, 16, part + HEAD),
            bf(planes, 16, part),
            bf(planes, 16, part + HEAD),
            bf(planes, 16, part),
            bf(PLANE, 16, part + HEAD),
            bf(PLANE, 16, part),
            bf(PLANE, 16, part + HEAD),
            bf(PLANE, 16, part),
            bf(PLANE, 16, 2 * HEAD),
            bf(PLANE, 16, 2 * HEAD),
            bf(planes, 16, 2 * HEAD),
            bf(planes, 16, 2 * HEAD),
            bf(adapters, rank, 2 * HEAD),
            bf(tps, rank, 2 * HEAD),
            bf(slots, HEAD),
            bf(tps - 1, slots, HEAD),
        ]
        + [bf(BLOCKS, rows, 2 * HEAD)] * 6
        + [
            bf(total, rank),
            fl(total, 2 * HEAD),
            fl(2 * rows, HEAD),
            fl(2 * decodes, HEAD),
            fl(16, 2 * HEAD),
            fl(decodes, HEAD),
            fl(groups, GROUP * heads, HEAD),
            fl(groups, GROUP * heads, HEAD),
            fl(groups, GROUP * heads, HEAD),
            dma((BLOCKS + 2 * 4 + 4,)),
            dma((CHUNKS, planes)),
            dma((CHUNKS, planes)),
            dma((CHUNKS, PLANE)),
            dma((CHUNKS, PLANE)),
            dma((tps,)),
            dma((tps,)),
            dma((3, BLOCKS)),
            dma((3, BLOCKS)),
            dma((tps,)),
            dma((tps,)),
            dma((PLANE,)),
            dma((PLANE,)),
            dma((planes,)),
            dma((planes,)),
        ],
        compiler_params=pltpu.CompilerParams(
            collective_id=0, has_side_effects=True, vmem_limit_bytes=44 * 1024 * 1024
        ),
    )(
        normed_input_rows,
        key_projection_weight,
        value_projection_weight,
        jnp.swapaxes(adapter_down_factors, 1, 2),
        adapter_up_factors.reshape(-1, HEAD),
        request_owner_replica.reshape(1, -1),
        request_adapter_slot.reshape(1, -1),
        prefill_adapter_slot,
        prefill_first_row,
        context_length.reshape(1, -1),
        request_page_table.T,
        queries,
        rotated_cache_keys,
        paged_cache_values,
        jnp.asarray(trig(1, 128)),
        jnp.asarray(trig(PIECE, 64)),
    )
    return (
        decode_kv.reshape(decodes, 2, HEAD),
        prefill_kv.reshape(prefills, 2, HEAD),
        attended,
    )


def solution(mesh):
    in_specs = (
        P("rep", "tp"),
        P("tp", None),
        P("tp", None),
        P("rep", "tp", None),
        P("rep", None, None, "tp"),
        P("rep", None),
        P("rep"),
        P("rep"),
        P("rep"),
        P("rep"),
        P("rep", None),
        P("rep", "tp"),
        P("rep", None, "tp"),
        P("rep", None, "tp"),
    )
    out_specs = (P("rep", None, "tp"), P("rep", None, "tp"), P("rep", "tp"))
    return jax.shard_map(shards, mesh=mesh, in_specs=in_specs, out_specs=out_specs, check_vma=False)
```

time: 225 us -> 68.4 us (0.30)
  waiting for transfers between devices: 84.8 us -> 0 us
  Pallas kernels: 0 us -> 50.9 us
  starting transfers between devices: 42 us -> 0 us
  matrix products: 36 us -> 0 us
  blocking collectives: 14.1 us -> 0 us
  between operations: 15.4 us -> 1.96 us
  other arithmetic: 10.2 us -> 0 us
  local copies, waits for them, and re-layouts: 20.4 us -> 15.1 us
    all_to_all x4 -> x0, waiting for transfers between devices: 72.1 us -> none  [the longest x1 53 us: shards(): lax.all_to_all(up_rows.astype(jnp.bfloat16), 'rep', split_axis=0, concat_...]
    pallas_call x0 -> x1, Pallas kernels: none -> 50.9 us  [shards(): pl.pallas_call(kernel, out_shape=(jax.ShapeDtypeStruct((2 * decodes, HEAD...]
    all_to_all x4 -> x0, starting transfers between devices: 41.5 us -> none  [the longest x1 13 us: shards(): lax.all_to_all(send_slot, 'rep', split_axis=0, concat_axis=0, tiled=True)]
    dot_general x16 -> x0, matrix products: 36 us -> none  [the longest x1 6.51 us: shards(): jnp.dot(prefill_input_rows, value_projection_weight, preferred_element_ty...]
    psum x1 -> x0, blocking collectives: 14.1 us -> none  [shards(): low_rank = lax.psum(low_rank, 'tp')]
    reduce_scatter x4 -> x0, waiting for transfers between devices: 12.7 us -> none  [the longest x1 12.6 us: head_sums(): lax.psum_scatter(parts[2], 'tp', scatter_dimension=1, tiled=True)]
    unnamed x20 -> x29, local copies, waits for them, and re-layouts: 5.29 us -> 15.1 us
    convert_element_type x1 -> x0, local copies, waits for them, and re-layouts: 6.28 us -> none  [shards(): up_rows.astype(jnp.bfloat16)]
  transfers between devices with their start and end apart: 9 -> 0, of which waited for: 4 -> 0; matrix products, arithmetic and copies ran while one was open for 26% -> 0% of each run, Pallas kernels for 0% -> 0%
where the time goes in v1:
time: 68.4 us; the launch traced here: 68 us
  Pallas kernels  50.9 us (74%)
  local copies, waits for them, and re-layouts  15.1 us (22%)
  between operations  1.96 us (3%)
    pallas_call x1, Pallas kernels, shards(): pl.pallas_call(kernel, out_shape=(jax.ShapeDtypeStruct((2 * decodes, HEAD...  50.9 us
    unnamed x29, local copies, waits for them, and re-layouts  15.1 us

profile of v1, /device:TPU:1, one launch (start us, length us, event | category | flops | bytes accessed | tf_op | source)
XLA Modules:
  0.0 68.0 jit_solution(13370596771425802760)
XLA Ops:
  1.9 0.0 copy-start
  1.9 1.6 %copy-done = bf16[2048,512]{1,0:T(8,128)(2,1)S(1)} copy-done((bf16[2048,512]{1,0:T(8,128)(2,1)S(1)}, bf16[2048,512]{1,0:T(8,128)(2,1)}, u32[]{:S(2)}) %copy-start) | copy-done | bytes 2097176
  3.5 0.0 copy-start.1
  3.5 1.6 %copy-done.1 = bf16[2048,512]{1,0:T(8,128)(2,1)S(1)} copy-done((bf16[2048,512]{1,0:T(8,128)(2,1)S(1)}, bf16[2048,512]{1,0:T(8,128)(2,1)}, u32[]{:S(2)}) %copy-start.1) | copy-done | bytes 2097176
  5.1 0.0 copy-start.2
  5.1 1.2 %copy-done.2 = bf16[4,2048,64]{1,2,0:T(8,128)(2,1)S(1)} copy-done((bf16[4,2048,64]{1,2,0:T(8,128)(2,1)S(1)}, bf16[4,2048,64]{1,2,0:T(8,128)(2,1)}, u32[]{:S(2)}) %copy-start.2) | copy-done | bytes 1048600
  6.3 1.2 %copy-done.3 = bf16[256,16,128]{2,1,0:T(8,128)(2,1)S(1)} copy-done((bf16[256,16,128]{2,1,0:T(8,128)(2,1)S(1)}, bf16[256,16,128]{2,1,0:T(8,128)(2,1)}, u32[]{:S(2)}) %copy-start.3) | copy-done | bytes 1048600
  7.6 0.0 copy-start.4
  7.6 1.2 %copy-done.4 = bf16[256,16,128]{2,1,0:T(8,128)(2,1)S(1)} copy-done((bf16[256,16,128]{2,1,0:T(8,128)(2,1)S(1)}, bf16[256,16,128]{2,1,0:T(8,128)(2,1)}, u32[]{:S(2)}) %copy-start.4) | copy-done | bytes 1048600
  8.8 0.0 copy-start.5
  8.8 0.9 %copy-done.5 = bf16[4,64,2,128]{3,2,1,0:T(2,128)(2,1)S(1)} copy-done((bf16[4,64,2,128]{3,2,1,0:T(2,128)(2,1)S(1)}, bf16[4,64,2,128]{3,2,1,0:T(2,128)(2,1)}, u32[]{:S(2)}) %copy-start.5) | copy-done | bytes 131096
  9.7 0.0 copy-start.6
  9.7 0.9 %copy-done.6 = bf16[64,1024]{1,0:T(8,128)(2,1)S(1)} copy-done((bf16[64,1024]{1,0:T(8,128)(2,1)S(1)}, bf16[64,1024]{1,0:T(8,128)(2,1)}, u32[]{:S(2)}) %copy-start.6) | copy-done | bytes 131096
  10.6 0.9 %copy-done.7 = f32[128,256]{1,0:T(8,128)S(1)} copy-done((f32[128,256]{1,0:T(8,128)S(1)}, f32[128,256]{1,0:T(8,128)}, u32[]{:S(2)}) %copy-start.7) | copy-done | bytes 131096
  11.5 0.0 copy-start.8
  11.5 0.8 %copy-done.8 = f32[64,256]{1,0:T(8,128)S(1)} copy-done((f32[64,256]{1,0:T(8,128)S(1)}, f32[64,256]{1,0:T(8,128)}, u32[]{:S(2)}) %copy-start.8) | copy-done | bytes 65560
  12.3 0.7 copy-done.9
  13.0 0.7 copy-done.10
  13.7 0.7 copy-done.11
  14.3 0.7 copy-done.12
  15.0 50.9 %shard_map.175 = (bf16[128,128]{1,0:T(8,128)(2,1)S(1)}, bf16[1920,128]{1,0:T(8,128)(2,1)S(1)}, bf16[64,1024]{1,0:T(8,128)(2,1)S(1)}) custom-call(bf16[1024,2048]{1,0:T(8,128)(2,1)} %x_hbm.1, bf16[2048,512]{1,0:T(8,128)(2,1)S(1)} %copy-done, bf16[2048,512]{1,0:T(8,128)(2,1)S(1)} %copy-done.1, bf16[4,64,2048]{2,1,0:T(8,128)(2,1)S(1)} %bitcast.8, ...), custom_call_target="tpu_custom_call" | custom-call | tf_op jit(solution)/shard_map/pallas_call | solution.py:551
  65.9 0.6 copy.24
  66.5 0.8 %copy.25 = bf16[960,2,128]{2,1,0:T(2,128)(2,1)} copy(bf16[960,2,128]{2,1,0:T(2,128)(2,1)S(1)} %bitcast.9) | data formatting | bytes 983040
  67.3 0.7 copy.26
  (6 shorter events, 0.0 us)
Async XLA Ops:
  1.9 1.6 %copy-start = (bf16[2048,512]{1,0:T(8,128)(2,1)S(1)}, bf16[2048,512]{1,0:T(8,128)(2,1)}, u32[]{:S(2)}) copy-start(bf16[2048,512]{1,0:T(8,128)(2,1)} %wk_hbm.1) | copy-start | bytes 6291460
  3.5 1.6 %copy-start.1 = (bf16[2048,512]{1,0:T(8,128)(2,1)S(1)}, bf16[2048,512]{1,0:T(8,128)(2,1)}, u32[]{:S(2)}) copy-start(bf16[2048,512]{1,0:T(8,128)(2,1)} %wv_hbm.1) | copy-start | bytes 6291460
  5.1 1.2 %copy-start.2 = (bf16[4,2048,64]{1,2,0:T(8,128)(2,1)S(1)}, bf16[4,2048,64]{1,2,0:T(8,128)(2,1)}, u32[]{:S(2)}) copy-start(bf16[4,2048,64]{1,2,0:T(8,128)(2,1)} %param.19) | copy-start | bytes 3145732
  6.3 1.2 %copy-start.3 = (bf16[256,16,128]{2,1,0:T(8,128)(2,1)S(1)}, bf16[256,16,128]{2,1,0:T(8,128)(2,1)}, u32[]{:S(2)}) copy-start(bf16[256,16,128]{2,1,0:T(8,128)(2,1)} %kpool_hbm.1) | copy-start | bytes 3145732
  7.6 1.2 %copy-start.4 = (bf16[256,16,128]{2,1,0:T(8,128)(2,1)S(1)}, bf16[256,16,128]{2,1,0:T(8,128)(2,1)}, u32[]{:S(2)}) copy-start(bf16[256,16,128]{2,1,0:T(8,128)(2,1)} %vpool_hbm.1) | copy-start | bytes 3145732
  8.8 0.9 %copy-start.5 = (bf16[4,64,2,128]{3,2,1,0:T(2,128)(2,1)S(1)}, bf16[4,64,2,128]{3,2,1,0:T(2,128)(2,1)}, u32[]{:S(2)}) copy-start(bf16[4,64,2,128]{3,2,1,0:T(2,128)(2,1)} %param.20) | copy-start | bytes 393220
  9.7 0.9 %copy-start.6 = (bf16[64,1024]{1,0:T(8,128)(2,1)S(1)}, bf16[64,1024]{1,0:T(8,128)(2,1)}, u32[]{:S(2)}) copy-start(bf16[64,1024]{1,0:T(8,128)(2,1)} %q_hbm.1) | copy-start | bytes 393220
  10.6 0.9 %copy-start.7 = (f32[128,256]{1,0:T(8,128)S(1)}, f32[128,256]{1,0:T(8,128)}, u32[]{:S(2)}) copy-start(f32[128,256]{1,0:T(8,128)} %constant.4.clone.low_ref) | copy-start | bytes 393220
  11.5 0.8 %copy-start.8 = (f32[64,256]{1,0:T(8,128)S(1)}, f32[64,256]{1,0:T(8,128)}, u32[]{:S(2)}) copy-start(f32[64,256]{1,0:T(8,128)} %constant.5.clone.high_ref) | copy-start | bytes 196612
  12.3 0.7 %copy-start.9 = (s32[64,4]{0,1:T(4,128)S(1)}, s32[64,4]{0,1:T(4,128)}, u32[]{:S(2)}) copy-start(s32[64,4]{0,1:T(4,128)} %param.26) | copy-start | bytes 3076
  13.0 0.7 copy-start.10
  13.7 0.7 copy-start.11
  14.3 0.7 copy-start.12

commit v2 on v1

--- a/solution.py
+++ b/solution.py
@@ -46,6 +46,21 @@
     wk_hbm,
     wv_hbm,
     d_hbm,
+    up_hbm,
+    owner_hbm,
+    slot_hbm,
+    pslot_hbm,
+    pfirst_hbm,
+    length_hbm,
+    table_hbm,
+    q_hbm,
+    kpool_hbm,
+    vpool_hbm,
+    low_hbm,
+    high_hbm,
+    dec_out,
+    pre_out,
+    att_out,
     up_ref,
     owner_ref,
     slot_ref,
@@ -53,14 +68,8 @@
     pfirst_ref,
     length_ref,
     table_ref,
-    q_hbm,
-    kpool_hbm,
-    vpool_hbm,
     low_ref,
     high_ref,
-    dec_out,
-    pre_out,
-    att_out,
     x,
     w,
     d,
@@ -101,20 +110,14 @@
     l_s,
     o_s,
     load_sem,
-    z1s,
-    z1r,
-    p1s,
-    p1r,
+    ex_s,
+    ex_r,
     us,
     ur,
     ys,
     yr,
     ns,
     nr,
-    p2s,
-    p2r,
-    z2s,
-    z2r,
 ):
     t = lax.axis_index("tp")
     rep = lax.axis_index("rep")
@@ -126,7 +129,7 @@
     decodes = q.shape[0]
     slots = 2 * lax.axis_size("rep")
     width = x.shape[1] // CHUNKS
-    s1, r1, s2, r2 = (s1a, s1b), (r1a, r1b), (s2a, s2b), (r2a, r2b)
+    s1 = (s1a, s1b)
 
     barrier = pltpu.get_barrier_semaphore()
 
@@ -145,9 +148,15 @@
     def each(low, high, body):
         lax.fori_loop(low, high, lambda i, c: (body(i), c)[1], 0)
 
-    each(1, planes, lambda k: pl.semaphore_signal(barrier, inc=1, **at(z_of(k) * PLANE + p, t)))
-    each(1, PLANE, lambda k: pl.semaphore_signal(barrier, inc=1, **at(z * PLANE + p_of(k), t)))
-    each(1, tps, lambda k: pl.semaphore_signal(barrier, inc=1, **at(rep, t_of(k))))
+    def far_first(count):
+        return sorted(range(1, count), key=lambda k: -min(k, count - k))
+
+    for k in far_first(planes):
+        pl.semaphore_signal(barrier, inc=1, **at(z_of(k) * PLANE + p, t))
+    for k in far_first(PLANE):
+        pl.semaphore_signal(barrier, inc=1, **at(z * PLANE + p_of(k), t))
+    for k in far_first(tps):
+        pl.semaphore_signal(barrier, inc=1, **at(rep, t_of(k)))
 
     def load(source, target, k):
         return pltpu.make_async_copy(source, target, load_sem.at[k])
@@ -168,7 +177,30 @@
     d_load = load(d_hbm, d, k0 + 1)
     kpool_load = load(kpool_hbm, kpool, k0 + 2)
     vpool_load = load(vpool_hbm, vpool, k0 + 3)
-    x_load(0).start()
+    small = [
+        load(source, target, k0 + 4 + i)
+        for i, (source, target) in enumerate(
+            (
+                (owner_hbm, owner_ref),
+                (slot_hbm, slot_ref),
+                (length_hbm, length_ref),
+                (pslot_hbm, pslot_ref),
+                (up_hbm, up_ref),
+                (pfirst_hbm, pfirst_ref),
+                (low_hbm, low_ref),
+                (high_hbm, high_ref),
+                (table_hbm, table_ref),
+            )
+        )
+    ]
+    head_load = load(x_hbm.at[pl.ds(0, decodes)], x.at[pl.ds(0, decodes)], k0 + 4 + len(small))
+    for c in small[:3]:
+        c.start()
+    head_load.start()
+    for c in small[3:]:
+        c.start()
+    rest = pl.ds(decodes, rows - decodes)
+    load(x_hbm.at[rest], x.at[rest], 0).start()
     d_load.start()
     for c in w_load(2):
         c.start()
@@ -180,6 +212,9 @@
     for c in (q_load, kpool_load, vpool_load):
         c.start()
 
+    for c in small[:3]:
+        c.wait()
+
     eye = iota((decodes, decodes), 0) == iota((decodes, decodes), 1)
 
     def column(row):
@@ -190,23 +225,30 @@
     same = owner_col == owner_row
     before_col = iota(eye.shape, 1) < iota(eye.shape, 0)
     before_row = iota(eye.shape, 0) < iota(eye.shape, 1)
-    target_col = 2.0 * owner_col + jnp.sum(
-        jnp.where(same & before_col, 1.0, 0.0), axis=1, keepdims=True
+    rank_col = jnp.sum(jnp.where(same & before_col, 1.0, 0.0), axis=1, keepdims=True)
+    rank_row = jnp.sum(jnp.where(same & before_row, 1.0, 0.0), axis=0, keepdims=True)
+
+    def plane_first(owner, turn):
+        owner = owner.astype(jnp.int32)
+        return (owner & (PLANE - 1)) * 16 + (owner >> 3) * 2 + turn.astype(jnp.int32)
+
+    slot_of = iota((slots, decodes), 0)
+    placing = (
+        one_hot((2.0 * owner_row + rank_row).astype(jnp.int32) == slot_of),
+        one_hot(plane_first(owner_row, rank_row) == slot_of),
     )
-    target_row = 2.0 * owner_row + jnp.sum(
-        jnp.where(same & before_row, 1.0, 0.0), axis=0, keepdims=True
-    )
-    placing = one_hot(target_row == iota((slots, decodes), 0).astype(F32))
-    placing_back = one_hot(target_col == iota((decodes, slots), 1).astype(F32))
+    placing_back = one_hot(plane_first(owner_col, rank_col) == iota((decodes, slots), 1))
     codes = jnp.broadcast_to(column(slot_ref[...].astype(F32)) + 1.0, (decodes, HEAD)).astype(BF16)
     lens[...] = jnp.broadcast_to(column(length_ref[...].astype(F32)), (decodes, HEAD))
 
-    x_load(0).wait()
+    head_load.wait()
     for c in range(CHUNKS):
-        placed = mm(placing, x[0:decodes, c * width : (c + 1) * width]).astype(BF16)
+        placed = mm(placing[c], x[0:decodes, c * width : (c + 1) * width]).astype(BF16)
         s1[c][:, :, 0:width] = placed.reshape(planes, 16, width)
-    s1a[:, :, width : width + HEAD] = mm(placing, codes).astype(BF16).reshape(planes, 16, HEAD)
-
+    s1a[:, :, width : width + HEAD] = mm(placing[0], codes).astype(BF16).reshape(planes, 16, HEAD)
+
+    for c in small[3:5]:
+        c.wait()
     pairs = up_ref[...]
     count = pairs.shape[0] // 2
     pick = iota((count, 2 * count), 1) - 2 * iota((count, 2 * count), 0)
@@ -216,29 +258,33 @@
     selected = pslot_ref[0]
     ug[t] = uall[selected]
 
-    def z1_copy(c, k):
-        to = z_of(k)
-        return pltpu.make_async_remote_copy(
-            s1[c].at[to], r1[c].at[z], z1s.at[c, k], z1r.at[c, k], **at(to * PLANE + p, t)
-        )
-
-    def p1_copy(c, k):
-        to = p_of(k)
-        return pltpu.make_async_remote_copy(
-            s2[c].at[to], r2[c].at[p], p1s.at[c, k], p1r.at[c, k], **at(z * PLANE + to, t)
-        )
-
-    def p2_copy(k):
-        to = p_of(k)
-        return pltpu.make_async_remote_copy(
-            s3.at[to], r3.at[p], p2s.at[k], p2r.at[k], **at(z * PLANE + to, t)
-        )
-
-    def z2_copy(k):
-        to = z_of(k)
-        return pltpu.make_async_remote_copy(
-            s4.at[to], r4.at[z], z2s.at[k], z2r.at[k], **at(to * PLANE + p, t)
-        )
+    def copy(source, target, send, recv, where):
+        return pltpu.make_async_remote_copy(source, target, send, recv, **where)
+
+    class Exchange:
+        def __init__(self, sent, got, me, of, place, send, recv):
+            self.sent, self.got, self.me, self.send, self.recv = sent, got, me, send, recv
+            self.of, self.place = of, place
+
+        def start(self):
+            for k in far_first(PLANE):
+                to = self.of(k)
+                copy(self.sent.at[to], self.got.at[self.me], self.send, self.recv, self.place(to)).start()
+            self.got[self.me] = self.sent[self.me]
+
+        def all(self):
+            most = pl.ds(0, PLANE - 1)
+            return copy(self.sent.at[most], self.got.at[most], self.send, self.recv, self.place(self.of(1)))
+
+    def over_z(sent, got, k):
+        return Exchange(sent, got, z, z_of, lambda to: at(to * PLANE + p, t), ex_s.at[k], ex_r.at[k])
+
+    def over_plane(sent, got, k):
+        return Exchange(sent, got, p, p_of, lambda to: at(z * PLANE + to, t), ex_s.at[k], ex_r.at[k])
+
+    first_hop = (over_z(s1a, r1a, 0), over_plane(s1b, r1b, 1))
+    second_hop = (over_plane(s2a, r2a, 2), over_z(s2b, r2b, 3))
+    back_hop = (over_z(s3, r3, 4), over_plane(s4, r4, 5))
 
     def up_copy(k):
         return pltpu.make_async_remote_copy(
@@ -272,12 +318,13 @@
         )
 
     pl.semaphore_wait(barrier, planes - 1 + PLANE - 1 + tps - 1)
-    each(1, tps, lambda k: up_copy(k).start())
-    for c in range(CHUNKS):
-        each(1, planes, lambda k: z1_copy(c, k).start())
-    for c in range(CHUNKS):
-        r1[c][z] = s1[c][z]
-
+    first_hop[0].start()
+    first_hop[1].start()
+    for k in far_first(tps):
+        up_copy(k).start()
+
+    for c in small[5:8]:
+        c.wait()
     first = pfirst_ref[0]
     high = high_ref[pl.ds(lax.div(first, PIECE), 1), :]
     low = low_ref[pl.ds(lax.rem(first, PIECE), 1), :]
@@ -301,7 +348,6 @@
     d_load.wait()
     for c in w_load(2):
         c.wait()
-    each(1, tps, lambda k: up_copy(k).wait_recv())
 
     def part_of(b, j):
         here = pl.ds(pl.multiple_of(b * rows, rows), rows)
@@ -310,6 +356,10 @@
     def relay_step(b):
         here = pl.ds(pl.multiple_of(b * rows, rows), rows)
 
+        @pl.when(b == 0)
+        def _():
+            load(x_hbm.at[rest], x.at[rest], 0).wait()
+
         @pl.when(b > 0)
         def _():
             x_load(b).wait()
@@ -317,7 +367,14 @@
         low_rank = mt(x[here, :], d[selected])
         row = iota(low_rank.shape, 0) + b * rows
         lrp[here, :] = jnp.where(row >= decodes, low_rank, 0.0).astype(BF16)
-        sr[b] = part_of(b, 2).astype(BF16)
+        part = mm(x[here, :], w[2])
+
+        @pl.when(b == 0)
+        def _():
+            for k in far_first(tps):
+                up_copy(k).wait_recv()
+
+        sr[b] = (part + mm(lrp[here, :], ug[t_of(2)])).astype(BF16)
         relay_copy(b).start()
 
     def direct_step(b):
@@ -341,21 +398,21 @@
         for c in w_load(j):
             c.wait()
     each(0, BLOCKS, lambda i: direct_step(order(i)))
+
+    def forward(c):
+        first_hop[c].all().wait_recv()
+        moved = mm(swap, first_hop[c].got[...].reshape(slots, -1)).astype(BF16)
+        second_hop[c].sent[...] = moved.reshape(PLANE, 16, -1)
+        second_hop[c].start()
+
+    forward(1)
     each(0, BLOCKS, lambda i: sum_step(order(i)))
-
-    def forward(c):
-        each(1, planes, lambda k: z1_copy(c, k).wait_recv())
-        moved = mm(swap, r1[c][...].reshape(slots, -1)).astype(BF16)
-        s2[c][...] = moved.reshape(PLANE, 16, -1)
-        each(1, PLANE, lambda k: p1_copy(c, k).start())
-        r2[c][p] = s2[c][p]
-
     forward(0)
     for c in w_load(0):
         c.wait()
     each(0, BLOCKS, own_step)
 
-    for c in (q_load, kpool_load, vpool_load):
+    for c in (q_load, kpool_load, vpool_load, small[8]):
         c.wait()
     maxp, page = table_ref.shape[0], kpool.shape[1]
     span = maxp * page
@@ -393,14 +450,15 @@
         l_s[i] = jnp.broadcast_to(jnp.sum(weights, axis=1, keepdims=True), (GROUP * heads, HEAD))
 
     each(0, decodes // GROUP, cached)
-    forward(1)
-
-    partial = jnp.zeros((slots, d.shape[0] * rank), F32)
-    for c in range(CHUNKS):
-        each(1, PLANE, lambda k: p1_copy(c, k).wait_recv())
-        factors = d[:, :, c * width : (c + 1) * width].reshape(-1, width)
-        partial = partial + mt(r2[c][:, :, 0:width].reshape(slots, width), factors)
-    code = r2a[:, :, width : width + HEAD].reshape(slots, HEAD).astype(F32)
+    def factors_of(c):
+        return d[:, :, c * width : (c + 1) * width].reshape(-1, width)
+
+    second_hop[0].all().wait_recv()
+    got = mm(swap, r2a[...].reshape(slots, -1)).astype(BF16)
+    partial = mt(got[:, 0:width], factors_of(0))
+    code = got[:, width:].astype(F32)
+    second_hop[1].all().wait_recv()
+    partial = partial + mt(r2b[...].reshape(slots, width), factors_of(1))
     lane_slot = (iota((slots, HEAD), 1) >> 6) + 1
     lane_slot = lane_slot.astype(F32)
     low_half = code == lane_slot
@@ -409,7 +467,8 @@
         high_half, partial[:, HEAD:], 0.0
     )
     ysend[...] = mine.astype(BF16)
-    each(1, tps, lambda k: low_copy(k).start())
+    for k in far_first(tps):
+        low_copy(k).start()
 
     sign = jnp.where(iota((1, HEAD), 1) < HALF, -1.0, 1.0)
 
@@ -437,9 +496,9 @@
         pre_out[begin : begin + 2 * rows - skip, :] = stage[skip:, :].astype(BF16)
 
     finish(0)
-    finish(2)
-
-    each(1, tps, lambda k: low_copy(k).wait_recv())
+
+    for k in far_first(tps):
+        low_copy(k).wait_recv()
     whole = mine
     for k in range(3):
         whole = whole + yrecv[k].astype(F32)
@@ -450,16 +509,15 @@
     fine = (wide - coarse.astype(F32)).astype(BF16)
     factors = uall[...].reshape(-1, 2 * HEAD)
     delta = mm(coarse, factors) + mm(fine, factors)
-    s3[...] = delta.astype(BF16).reshape(PLANE, 16, 2 * HEAD)
-    each(1, PLANE, lambda k: p2_copy(k).start())
-    r3[p] = s3[p]
-
+    s3[...] = delta.astype(BF16).reshape(planes, 16, 2 * HEAD)
+    back_hop[0].start()
+
+    finish(2)
     finish(1)
 
-    each(1, PLANE, lambda k: p2_copy(k).wait_recv())
-    s4[...] = mm(swap, r3[...].reshape(slots, -1)).astype(BF16).reshape(planes, 16, -1)
-    each(1, planes, lambda k: z2_copy(k).start())
-    r4[z] = s4[z]
+    back_hop[0].all().wait_recv()
+    s4[...] = mm(swap, r3[...].reshape(slots, -1)).astype(BF16).reshape(PLANE, 16, -1)
+    back_hop[1].start()
 
     finish(3)
 
@@ -471,7 +529,7 @@
         precision=lax.Precision.HIGHEST,
         preferred_element_type=F32,
     )
-    each(1, planes, lambda k: z2_copy(k).wait_recv())
+    back_hop[1].all().wait_recv()
     both = own[0:decodes, :] + mm(placing_back, r4[...].reshape(slots, -1))
     keys = rotated(both[:, 0:HEAD], angles[:, 0:HEAD], angles[:, HEAD:]).astype(BF16).astype(F32)
     values = both[:, HEAD:].astype(BF16).astype(F32)
@@ -492,13 +550,11 @@
                 g * GROUP : (g + 1) * GROUP
             ].astype(BF16)
 
-    for c in range(CHUNKS):
-        each(1, planes, lambda k: z1_copy(c, k).wait_send())
-        each(1, PLANE, lambda k: p1_copy(c, k).wait_send())
-    each(1, planes, lambda k: z2_copy(k).wait_send())
-    each(1, PLANE, lambda k: p2_copy(k).wait_send())
-    each(1, tps, lambda k: up_copy(k).wait_send())
-    each(1, tps, lambda k: low_copy(k).wait_send())
+    for hop in first_hop + second_hop + back_hop:
+        hop.all().wait_send()
+    for k in far_first(tps):
+        up_copy(k).wait_send()
+        low_copy(k).wait_send()
 
     def sent(b):
         relay_copy(b).wait_send()
@@ -538,8 +594,7 @@
     heads = queries.shape[1] // HEAD
     span = decodes * request_page_table.shape[1] * page
     vmem = pl.BlockSpec(memory_space=pltpu.VMEM)
-    smem = pl.BlockSpec(memory_space=pltpu.SMEM)
-    hbm = pl.BlockSpec(memory_space=pl.ANY)
+    hbm = pl.BlockSpec(memory_space=pltpu.HBM)
     dma = pltpu.SemaphoreType.DMA
 
     def bf(*shape):
@@ -555,9 +610,18 @@
             jax.ShapeDtypeStruct((2 * prefills, HEAD), BF16),
             jax.ShapeDtypeStruct(queries.shape, BF16),
         ),
-        in_specs=[hbm, hbm, hbm, hbm, vmem, vmem, vmem, smem, smem, vmem, smem, hbm, hbm, hbm, vmem, vmem],
+        in_specs=[hbm] * 16,
         out_specs=(vmem, vmem, vmem),
         scratch_shapes=[
+            bf(2 * adapters * rank, HEAD),
+            pltpu.VMEM((1, decodes), jnp.int32),
+            pltpu.VMEM((1, decodes), jnp.int32),
+            pltpu.SMEM((1,), jnp.int32),
+            pltpu.SMEM((1,), jnp.int32),
+            pltpu.VMEM((1, decodes), jnp.int32),
+            pltpu.SMEM(request_page_table.shape[::-1], jnp.int32),
+            fl(128, 2 * HEAD),
+            fl(64, 2 * HEAD),
             bf(total, width),
             bf(tps, width, 2 * HEAD),
             bf(adapters, rank, width),
@@ -594,24 +658,18 @@
             fl(groups, GROUP * heads, HEAD),
             fl(groups, GROUP * heads, HEAD),
             fl(groups, GROUP * heads, HEAD),
-            dma((BLOCKS + 2 * 4 + 4,)),
-            dma((CHUNKS, planes)),
-            dma((CHUNKS, planes)),
-            dma((CHUNKS, PLANE)),
-            dma((CHUNKS, PLANE)),
+            dma((BLOCKS + 2 * 4 + 4 + 10,)),
+            dma((6,)),
+            dma((6,)),
             dma((tps,)),
             dma((tps,)),
             dma((3, BLOCKS)),
             dma((3, BLOCKS)),
             dma((tps,)),
             dma((tps,)),
-            dma((PLANE,)),
-            dma((PLANE,)),
-            dma((planes,)),
-            dma((planes,)),
         ],
         compiler_params=pltpu.CompilerParams(
-            collective_id=0, has_side_effects=True, vmem_limit_bytes=44 * 1024 * 1024
+            collective_id=0, has_side_effects=True, vmem_limit_bytes=60 * 1024 * 1024
         ),
     )(
         normed_input_rows,

time: 68.4 us -> 53 us (0.77)
  local copies, waits for them, and re-layouts: 15.1 us -> 5.11 us
  Pallas kernels: 50.9 us -> 45.7 us
    unnamed x29 -> x3, local copies, waits for them, and re-layouts: 15.1 us -> 5.11 us
    pallas_call x1, Pallas kernels: 50.9 us -> 45.7 us  [shards(): pl.pallas_call(kernel, out_shape=(jax.ShapeDtypeStruct((2 * decodes, HEAD...]
where the time goes in v2:
time: 53 us; the launch traced here: 52.8 us
  Pallas kernels  45.7 us (86%)
  local copies, waits for them, and re-layouts  5.11 us (10%)
  between operations  1.93 us (4%)
    pallas_call x1, Pallas kernels, shards(): pl.pallas_call(kernel, out_shape=(jax.ShapeDtypeStruct((2 * decodes, HEAD...  45.7 us
    unnamed x3, local copies, waits for them, and re-layouts  5.11 us

profile of v2, /device:TPU:1, one launch (start us, length us, event | category | flops | bytes accessed | tf_op | source)
XLA Modules:
  0.0 52.8 jit_solution(10425363457347103644)
XLA Ops:
  1.9 45.7 %shard_map.175 = (bf16[128,128]{1,0:T(8,128)(2,1)}, bf16[1920,128]{1,0:T(8,128)(2,1)}, bf16[64,1024]{1,0:T(8,128)(2,1)}) custom-call(bf16[1024,2048]{1,0:T(8,128)(2,1)} %x_hbm.1, bf16[2048,512]{1,0:T(8,128)(2,1)} %wk_hbm.1, bf16[2048,512]{1,0:T(8,128)(2,1)} %wv_hbm.1, bf16[4,64,2048]{2,1,0:T(8,128)(2,1)} %bitcast.8, bf16[512,128]{1,0:T(8,128)(2,1)} %bitcast.10, ...), custom_call_target="tpu_custom_call" | custom-call | tf_op jit(solution)/shard_map/pallas_call | solution.py:606
  47.7 1.4 %copy.24 = bf16[64,2,128]{2,1,0:T(2,128)(2,1)} copy(bf16[64,2,128]{2,1,0:T(2,128)(2,1)} %bitcast.11) | data formatting | bytes 65536
  49.1 2.1 %copy.25 = bf16[960,2,128]{2,1,0:T(2,128)(2,1)} copy(bf16[960,2,128]{2,1,0:T(2,128)(2,1)} %bitcast.9) | data formatting | bytes 983040
  51.2 1.6 %copy.26 = bf16[64,1024]{1,0:T(8,128)(2,1)} copy(bf16[64,1024]{1,0:T(8,128)(2,1)} %get-tuple-element.14) | data formatting | bytes 262144

commit v3 on v2

--- a/solution.py
+++ b/solution.py
@@ -104,6 +104,9 @@
     own,
     stage,
     dec,
+    dec_half,
+    pre,
+    att,
     base,
     lens,
     m_s,
@@ -367,14 +370,11 @@
         low_rank = mt(x[here, :], d[selected])
         row = iota(low_rank.shape, 0) + b * rows
         lrp[here, :] = jnp.where(row >= decodes, low_rank, 0.0).astype(BF16)
-        part = mm(x[here, :], w[2])
-
-        @pl.when(b == 0)
-        def _():
-            for k in far_first(tps):
-                up_copy(k).wait_recv()
-
-        sr[b] = (part + mm(lrp[here, :], ug[t_of(2)])).astype(BF16)
+        own[here, :] = mm(x[here, :], w[2])
+
+    def relay_send(b):
+        here = pl.ds(pl.multiple_of(b * rows, rows), rows)
+        sr[b] = (own[here, :] + mm(lrp[here, :], ug[t_of(2)])).astype(BF16)
         relay_copy(b).start()
 
     def direct_step(b):
@@ -385,7 +385,6 @@
         part = part_of(b, ahead(b))
         relay_copy(b).wait_recv()
         sc[b] = (part + rr[b].astype(F32)).astype(BF16)
-        sum_copy(b).start()
 
     def own_step(b):
         own[pl.ds(pl.multiple_of(b * rows, rows), rows), :] = part_of(b, 0)
@@ -394,10 +393,13 @@
         return lax.div(i, 2) + 2 * lax.rem(i, 2)
 
     each(0, BLOCKS, lambda i: relay_step(order(i)))
+    for k in far_first(tps):
+        up_copy(k).wait_recv()
+    each(0, BLOCKS, lambda i: relay_send(order(i)))
     for j in (3, 1):
         for c in w_load(j):
             c.wait()
-    each(0, BLOCKS, lambda i: direct_step(order(i)))
+    each(0, 2, lambda i: direct_step(order(i)))
 
     def forward(c):
         first_hop[c].all().wait_recv()
@@ -406,7 +408,10 @@
         second_hop[c].start()
 
     forward(1)
+    each(2, BLOCKS, lambda i: direct_step(order(i)))
     each(0, BLOCKS, lambda i: sum_step(order(i)))
+    for b in (0, 2):
+        sum_copy(b).start()
     forward(0)
     for c in w_load(0):
         c.wait()
@@ -469,7 +474,10 @@
     ysend[...] = mine.astype(BF16)
     for k in far_first(tps):
         low_copy(k).start()
-
+    for b in (1, 3):
+        sum_copy(b).start()
+
+    written = []
     sign = jnp.where(iota((1, HEAD), 1) < HALF, -1.0, 1.0)
 
     def rotated(keys, cosine, sine):
@@ -493,9 +501,13 @@
             stage[pl.ds(2 * i * PIECE + 1, PIECE, stride=2), :] = piece[:, HEAD:]
         skip = 2 * PIECE if b == 0 else 0
         begin = 2 * (b * rows - decodes) + skip
-        pre_out[begin : begin + 2 * rows - skip, :] = stage[skip:, :].astype(BF16)
+        pre[begin : begin + 2 * rows - skip, :] = stage[skip:, :].astype(BF16)
+        here = pl.ds(begin, 2 * rows - skip)
+        written.append(load(pre.at[here], pre_out.at[here], b))
+        written[-1].start()
 
     finish(0)
+    finish(2)
 
     for k in far_first(tps):
         low_copy(k).wait_recv()
@@ -512,14 +524,12 @@
     s3[...] = delta.astype(BF16).reshape(planes, 16, 2 * HEAD)
     back_hop[0].start()
 
-    finish(2)
     finish(1)
+    finish(3)
 
     back_hop[0].all().wait_recv()
     s4[...] = mm(swap, r3[...].reshape(slots, -1)).astype(BF16).reshape(PLANE, 16, -1)
     back_hop[1].start()
-
-    finish(3)
 
     chosen = lens[:, 0:1] == iota((decodes, low_ref.shape[0]), 1).astype(F32)
     angles = lax.dot_general(
@@ -535,7 +545,9 @@
     values = both[:, HEAD:].astype(BF16).astype(F32)
     dec[pl.ds(0, decodes, stride=2), :] = keys
     dec[pl.ds(1, decodes, stride=2), :] = values
-    dec_out[...] = dec[...].astype(BF16)
+    dec_half[...] = dec[...].astype(BF16)
+    written.append(load(dec_half, dec_out, BLOCKS))
+    written[-1].start()
     for i in range(decodes // GROUP):
         key = jnp.concatenate([keys[i * GROUP : (i + 1) * GROUP]] * heads, axis=0)
         value = jnp.concatenate([values[i * GROUP : (i + 1) * GROUP]] * heads, axis=0)
@@ -546,9 +558,11 @@
         share = jnp.exp(score - top)
         result = (o_s[i] * shrink + share * value) / (l_s[i] * shrink + share)
         for g in range(heads):
-            att_out[i * GROUP : (i + 1) * GROUP, g * HEAD : (g + 1) * HEAD] = result[
+            att[i * GROUP : (i + 1) * GROUP, g * HEAD : (g + 1) * HEAD] = result[
                 g * GROUP : (g + 1) * GROUP
             ].astype(BF16)
+    written.append(load(att, att_out, BLOCKS + 1))
+    written[-1].start()
 
     for hop in first_hop + second_hop + back_hop:
         hop.all().wait_send()
@@ -562,6 +576,21 @@
         sum_copy(b).wait_send()
 
     each(0, BLOCKS, sent)
+    for c in written:
+        c.wait()
+
+
+def hand_over(dec, pre, att, dec_out, pre_out, att_out, pre_held, att_held, dec_held, sem):
+    ways = ((pre, pre_held, pre_out), (att, att_held, att_out), (dec, dec_held, dec_out))
+    fetched = [pltpu.make_async_copy(a, b, sem.at[0, i]) for i, (a, b, _) in enumerate(ways)]
+    written = [pltpu.make_async_copy(b, c, sem.at[1, i]) for i, (_, b, c) in enumerate(ways)]
+    for c in fetched:
+        c.start()
+    for c, e in zip(fetched, written):
+        c.wait()
+        e.start()
+    for e in written:
+        e.wait()
 
 
 def shards(
@@ -593,7 +622,6 @@
     groups = decodes // GROUP
     heads = queries.shape[1] // HEAD
     span = decodes * request_page_table.shape[1] * page
-    vmem = pl.BlockSpec(memory_space=pltpu.VMEM)
     hbm = pl.BlockSpec(memory_space=pltpu.HBM)
     dma = pltpu.SemaphoreType.DMA
 
@@ -611,7 +639,7 @@
             jax.ShapeDtypeStruct(queries.shape, BF16),
         ),
         in_specs=[hbm] * 16,
-        out_specs=(vmem, vmem, vmem),
+        out_specs=(hbm, hbm, hbm),
         scratch_shapes=[
             bf(2 * adapters * rank, HEAD),
             pltpu.VMEM((1, decodes), jnp.int32),
@@ -653,6 +681,9 @@
             fl(total, 2 * HEAD),
             fl(2 * rows, HEAD),
             fl(2 * decodes, HEAD),
+            bf(2 * decodes, HEAD),
+            bf(2 * prefills, HEAD),
+            bf(*queries.shape),
             fl(16, 2 * HEAD),
             fl(decodes, HEAD),
             fl(groups, GROUP * heads, HEAD),
@@ -689,6 +720,14 @@
         jnp.asarray(trig(1, 128)),
         jnp.asarray(trig(PIECE, 64)),
     )
+    decode_kv, prefill_kv, attended = pl.pallas_call(
+        hand_over,
+        out_shape=tuple(jax.ShapeDtypeStruct(a.shape, BF16) for a in (decode_kv, prefill_kv, attended)),
+        in_specs=[hbm] * 3,
+        out_specs=(hbm,) * 3,
+        scratch_shapes=[bf(*a.shape) for a in (prefill_kv, attended, decode_kv)] + [dma((2, 3))],
+        compiler_params=pltpu.CompilerParams(vmem_limit_bytes=60 * 1024 * 1024),
+    )(decode_kv, prefill_kv, attended)
     return (
         decode_kv.reshape(decodes, 2, HEAD),
         prefill_kv.reshape(prefills, 2, HEAD),

time: 53 us -> 47.9 us (0.904)
  local copies, waits for them, and re-layouts: 5.11 us -> 0 us
    unnamed x3 -> x0, local copies, waits for them, and re-layouts: 5.11 us -> none
    pallas_call x0 -> x1, Pallas kernels: none -> 1.9 us  [shards(): pl.pallas_call(hand_over, out_shape=tuple((jax.ShapeDtypeStruct(a.shape,...]
    pallas_call x1, Pallas kernels: 45.7 us -> 43.9 us  [shards(): pl.pallas_call(kernel, out_shape=(jax.ShapeDtypeStruct((2 * decodes, HEAD...]
where the time goes in v3:
time: 47.9 us; the launch traced here: 47.7 us
  Pallas kernels  45.8 us (96%)
  between operations  1.93 us (4%)
    pallas_call x1, Pallas kernels, shards(): pl.pallas_call(kernel, out_shape=(jax.ShapeDtypeStruct((2 * decodes, HEAD...  43.9 us
    pallas_call x1, Pallas kernels, shards(): pl.pallas_call(hand_over, out_shape=tuple((jax.ShapeDtypeStruct(a.shape,...  1.9 us

profile of v3, /device:TPU:1, one launch (start us, length us, event | category | flops | bytes accessed | tf_op | source)
XLA Modules:
  0.0 47.7 jit_solution(14161524010282767171)
XLA Ops:
  1.9 43.9 %shard_map.175 = (bf16[128,128]{1,0:T(8,128)(2,1)}, bf16[1920,128]{1,0:T(8,128)(2,1)}, bf16[64,1024]{1,0:T(8,128)(2,1)}) custom-call(bf16[1024,2048]{1,0:T(8,128)(2,1)} %x_hbm.1, bf16[2048,512]{1,0:T(8,128)(2,1)} %wk_hbm.1, bf16[2048,512]{1,0:T(8,128)(2,1)} %wv_hbm.1, bf16[4,64,2048]{2,1,0:T(8,128)(2,1)} %bitcast.8, bf16[512,128]{1,0:T(8,128)(2,1)} %bitcast.9, ...), custom_call_target="tpu_custom_call" | custom-call | tf_op jit(solution)/shard_map/pallas_call | solution.py:634
  45.8 1.9 %shard_map.176 = (bf16[128,128]{1,0:T(8,128)(2,1)}, bf16[1920,128]{1,0:T(8,128)(2,1)}, bf16[64,1024]{1,0:T(8,128)(2,1)}) custom-call(bf16[128,128]{1,0:T(8,128)(2,1)} %get-tuple-element.9.dec, bf16[1920,128]{1,0:T(8,128)(2,1)} %get-tuple-element.10.pre, bf16[64,1024]{1,0:T(8,128)(2,1)} %get-tuple-element.11.att), custom_call_target="tpu_custom_call" | custom-call | tf_op jit(solution)/shard_map/pallas_call | solution.py:723

commit v4 on v3

--- a/solution.py
+++ b/solution.py
@@ -154,13 +154,6 @@
     def far_first(count):
         return sorted(range(1, count), key=lambda k: -min(k, count - k))
 
-    for k in far_first(planes):
-        pl.semaphore_signal(barrier, inc=1, **at(z_of(k) * PLANE + p, t))
-    for k in far_first(PLANE):
-        pl.semaphore_signal(barrier, inc=1, **at(z * PLANE + p_of(k), t))
-    for k in far_first(tps):
-        pl.semaphore_signal(barrier, inc=1, **at(rep, t_of(k)))
-
     def load(source, target, k):
         return pltpu.make_async_copy(source, target, load_sem.at[k])
 
@@ -197,9 +190,16 @@
         )
     ]
     head_load = load(x_hbm.at[pl.ds(0, decodes)], x.at[pl.ds(0, decodes)], k0 + 4 + len(small))
-    for c in small[:3]:
+    small[0].start()
+    head_load.start()
+    for c in small[1:3]:
         c.start()
-    head_load.start()
+    for k in far_first(planes):
+        pl.semaphore_signal(barrier, inc=1, **at(z_of(k) * PLANE + p, t))
+    for k in far_first(PLANE):
+        pl.semaphore_signal(barrier, inc=1, **at(z * PLANE + p_of(k), t))
+    for k in far_first(tps):
+        pl.semaphore_signal(barrier, inc=1, **at(rep, t_of(k)))
     for c in small[3:]:
         c.start()
     rest = pl.ds(decodes, rows - decodes)
@@ -242,13 +242,75 @@
     )
     placing_back = one_hot(plane_first(owner_col, rank_col) == iota((decodes, slots), 1))
     codes = jnp.broadcast_to(column(slot_ref[...].astype(F32)) + 1.0, (decodes, HEAD)).astype(BF16)
-    lens[...] = jnp.broadcast_to(column(length_ref[...].astype(F32)), (decodes, HEAD))
 
     head_load.wait()
     for c in range(CHUNKS):
         placed = mm(placing[c], x[0:decodes, c * width : (c + 1) * width]).astype(BF16)
         s1[c][:, :, 0:width] = placed.reshape(planes, 16, width)
     s1a[:, :, width : width + HEAD] = mm(placing[0], codes).astype(BF16).reshape(planes, 16, HEAD)
+
+    def copy(source, target, send, recv, where):
+        return pltpu.make_async_remote_copy(source, target, send, recv, **where)
+
+    class Exchange:
+        def __init__(self, sent, got, me, of, place, send, recv):
+            self.sent, self.got, self.me, self.send, self.recv = sent, got, me, send, recv
+            self.of, self.place = of, place
+
+        def start(self):
+            for k in far_first(PLANE):
+                to = self.of(k)
+                copy(self.sent.at[to], self.got.at[self.me], self.send, self.recv, self.place(to)).start()
+            self.got[self.me] = self.sent[self.me]
+
+        def all(self):
+            most = pl.ds(0, PLANE - 1)
+            return copy(self.sent.at[most], self.got.at[most], self.send, self.recv, self.place(self.of(1)))
+
+    def over_z(sent, got, k):
+        return Exchange(sent, got, z, z_of, lambda to: at(to * PLANE + p, t), ex_s.at[k], ex_r.at[k])
+
+    def over_plane(sent, got, k):
+        return Exchange(sent, got, p, p_of, lambda to: at(z * PLANE + to, t), ex_s.at[k], ex_r.at[k])
+
+    first_hop = (over_z(s1a, r1a, 0), over_plane(s1b, r1b, 1))
+    second_hop = (over_plane(s2a, r2a, 2), over_z(s2b, r2b, 3))
+    back_hop = (over_z(s3, r3, 4), over_plane(s4, r4, 5))
+
+    def up_copy(k):
+        return pltpu.make_async_remote_copy(
+            ug.at[t], ug.at[t], us.at[k], ur.at[k], **at(rep, t_of(k))
+        )
+
+    def low_copy(k):
+        return pltpu.make_async_remote_copy(
+            ysend, yrecv.at[k - 1], ns.at[k], nr.at[k], **at(rep, t_of(k))
+        )
+
+    def ahead(b):
+        return 1 + 2 * lax.div(b, 2)
+
+    def back(b):
+        return 3 - 2 * lax.div(b, 2)
+
+    def relay_copy(b):
+        return pltpu.make_async_remote_copy(
+            sr.at[b], rr.at[b], ys.at[0, b], yr.at[0, b], **at(rep, t_of(ahead(b)))
+        )
+
+    def direct_copy(b):
+        return pltpu.make_async_remote_copy(
+            sd.at[b], rd.at[b], ys.at[1, b], yr.at[1, b], **at(rep, t_of(back(b)))
+        )
+
+    def sum_copy(b):
+        return pltpu.make_async_remote_copy(
+            sc.at[b], rc.at[b], ys.at[2, b], yr.at[2, b], **at(rep, t_of(ahead(b)))
+        )
+
+    pl.semaphore_wait(barrier, planes - 1 + PLANE - 1 + tps - 1)
+    first_hop[0].start()
+    first_hop[1].start()
 
     for c in small[3:5]:
         c.wait()
@@ -260,71 +322,10 @@
     uall[:, :, HEAD:] = mm(one_hot(pick == 1), pairs).astype(BF16).reshape(-1, rank, HEAD)
     selected = pslot_ref[0]
     ug[t] = uall[selected]
-
-    def copy(source, target, send, recv, where):
-        return pltpu.make_async_remote_copy(source, target, send, recv, **where)
-
-    class Exchange:
-        def __init__(self, sent, got, me, of, place, send, recv):
-            self.sent, self.got, self.me, self.send, self.recv = sent, got, me, send, recv
-            self.of, self.place = of, place
-
-        def start(self):
-            for k in far_first(PLANE):
-                to = self.of(k)
-                copy(self.sent.at[to], self.got.at[self.me], self.send, self.recv, self.place(to)).start()
-            self.got[self.me] = self.sent[self.me]
-
-        def all(self):
-            most = pl.ds(0, PLANE - 1)
-            return copy(self.sent.at[most], self.got.at[most], self.send, self.recv, self.place(self.of(1)))
-
-    def over_z(sent, got, k):
-        return Exchange(sent, got, z, z_of, lambda to: at(to * PLANE + p, t), ex_s.at[k], ex_r.at[k])
-
-    def over_plane(sent, got, k):
-        return Exchange(sent, got, p, p_of, lambda to: at(z * PLANE + to, t), ex_s.at[k], ex_r.at[k])
-
-    first_hop = (over_z(s1a, r1a, 0), over_plane(s1b, r1b, 1))
-    second_hop = (over_plane(s2a, r2a, 2), over_z(s2b, r2b, 3))
-    back_hop = (over_z(s3, r3, 4), over_plane(s4, r4, 5))
-
-    def up_copy(k):
-        return pltpu.make_async_remote_copy(
-            ug.at[t], ug.at[t], us.at[k], ur.at[k], **at(rep, t_of(k))
-        )
-
-    def low_copy(k):
-        return pltpu.make_async_remote_copy(
-            ysend, yrecv.at[k - 1], ns.at[k], nr.at[k], **at(rep, t_of(k))
-        )
-
-    def ahead(b):
-        return 1 + 2 * lax.div(b, 2)
-
-    def back(b):
-        return 3 - 2 * lax.div(b, 2)
-
-    def relay_copy(b):
-        return pltpu.make_async_remote_copy(
-            sr.at[b], rr.at[b], ys.at[0, b], yr.at[0, b], **at(rep, t_of(ahead(b)))
-        )
-
-    def direct_copy(b):
-        return pltpu.make_async_remote_copy(
-            sd.at[b], rd.at[b], ys.at[1, b], yr.at[1, b], **at(rep, t_of(back(b)))
-        )
-
-    def sum_copy(b):
-        return pltpu.make_async_remote_copy(
-            sc.at[b], rc.at[b], ys.at[2, b], yr.at[2, b], **at(rep, t_of(ahead(b)))
-        )
-
-    pl.semaphore_wait(barrier, planes - 1 + PLANE - 1 + tps - 1)
-    first_hop[0].start()
-    first_hop[1].start()
     for k in far_first(tps):
         up_copy(k).start()
+
+    lens[...] = jnp.broadcast_to(column(length_ref[...].astype(F32)), (decodes, HEAD))
 
     for c in small[5:8]:
         c.wait()
@@ -409,13 +410,12 @@
 
     forward(1)
     each(2, BLOCKS, lambda i: direct_step(order(i)))
-    each(0, BLOCKS, lambda i: sum_step(order(i)))
-    for b in (0, 2):
-        sum_copy(b).start()
-    forward(0)
     for c in w_load(0):
         c.wait()
     each(0, BLOCKS, own_step)
+    each(0, 2, lambda i: sum_step(order(i)))
+    forward(0)
+    each(2, BLOCKS, lambda i: sum_step(order(i)))
 
     for c in (q_load, kpool_load, vpool_load, small[8]):
         c.wait()
@@ -474,7 +474,7 @@
     ysend[...] = mine.astype(BF16)
     for k in far_first(tps):
         low_copy(k).start()
-    for b in (1, 3):
+    for b in (0, 2, 1, 3):
         sum_copy(b).start()
 
     written = []
@@ -506,9 +506,6 @@
         written.append(load(pre.at[here], pre_out.at[here], b))
         written[-1].start()
 
-    finish(0)
-    finish(2)
-
     for k in far_first(tps):
         low_copy(k).wait_recv()
     whole = mine
@@ -524,12 +521,12 @@
     s3[...] = delta.astype(BF16).reshape(planes, 16, 2 * HEAD)
     back_hop[0].start()
 
-    finish(1)
-    finish(3)
-
     back_hop[0].all().wait_recv()
     s4[...] = mm(swap, r3[...].reshape(slots, -1)).astype(BF16).reshape(PLANE, 16, -1)
     back_hop[1].start()
+
+    for b in (0, 2, 1, 3):
+        finish(b)
 
     chosen = lens[:, 0:1] == iota((decodes, low_ref.shape[0]), 1).astype(F32)
     angles = lax.dot_general(

time: 47.9 us -> 46.1 us (0.962)
  Pallas kernels: 45.8 us -> 44 us
    pallas_call x1, Pallas kernels: 43.9 us -> 42.1 us  [shards(): pl.pallas_call(kernel, out_shape=(jax.ShapeDtypeStruct((2 * decodes, HEAD...]
where the time goes in v4:
time: 46.1 us; the launch traced here: 46 us
  Pallas kernels  44 us (95%)
  between operations  1.93 us (4%)
    pallas_call x1, Pallas kernels, shards(): pl.pallas_call(kernel, out_shape=(jax.ShapeDtypeStruct((2 * decodes, HEAD...  42.1 us
    pallas_call x1, Pallas kernels, shards(): pl.pallas_call(hand_over, out_shape=tuple((jax.ShapeDtypeStruct(a.shape,...  1.9 us

profile of v4, /device:TPU:1, one launch (start us, length us, event | category | flops | bytes accessed | tf_op | source)
XLA Modules:
  0.0 46.0 jit_solution(8716678191414888721)
XLA Ops:
  1.9 42.1 %shard_map.175 = (bf16[128,128]{1,0:T(8,128)(2,1)}, bf16[1920,128]{1,0:T(8,128)(2,1)}, bf16[64,1024]{1,0:T(8,128)(2,1)}) custom-call(bf16[1024,2048]{1,0:T(8,128)(2,1)} %x_hbm.1, bf16[2048,512]{1,0:T(8,128)(2,1)} %wk_hbm.1, bf16[2048,512]{1,0:T(8,128)(2,1)} %wv_hbm.1, bf16[4,64,2048]{2,1,0:T(8,128)(2,1)} %bitcast.8, bf16[512,128]{1,0:T(8,128)(2,1)} %bitcast.9, ...), custom_call_target="tpu_custom_call" | custom-call | tf_op jit(solution)/shard_map/pallas_call | solution.py:631
  44.1 1.9 %shard_map.176 = (bf16[128,128]{1,0:T(8,128)(2,1)}, bf16[1920,128]{1,0:T(8,128)(2,1)}, bf16[64,1024]{1,0:T(8,128)(2,1)}) custom-call(bf16[128,128]{1,0:T(8,128)(2,1)} %get-tuple-element.9.dec, bf16[1920,128]{1,0:T(8,128)(2,1)} %get-tuple-element.10.pre, bf16[64,1024]{1,0:T(8,128)(2,1)} %get-tuple-element.11.att), custom_call_target="tpu_custom_call" | custom-call | tf_op jit(solution)/shard_map/pallas_call | solution.py:720

commit v5 on v4

--- a/solution.py
+++ b/solution.py
@@ -373,14 +373,12 @@
         lrp[here, :] = jnp.where(row >= decodes, low_rank, 0.0).astype(BF16)
         own[here, :] = mm(x[here, :], w[2])
 
-    def relay_send(b):
+    def relay_sum(b):
         here = pl.ds(pl.multiple_of(b * rows, rows), rows)
         sr[b] = (own[here, :] + mm(lrp[here, :], ug[t_of(2)])).astype(BF16)
-        relay_copy(b).start()
 
     def direct_step(b):
         sd[b] = part_of(b, back(b)).astype(BF16)
-        direct_copy(b).start()
 
     def sum_step(b):
         part = part_of(b, ahead(b))
@@ -396,7 +394,10 @@
     each(0, BLOCKS, lambda i: relay_step(order(i)))
     for k in far_first(tps):
         up_copy(k).wait_recv()
-    each(0, BLOCKS, lambda i: relay_send(order(i)))
+    each(0, 2, lambda i: relay_sum(order(i)))
+    for b in (0, 2):
+        relay_copy(b).start()
+    each(2, BLOCKS, lambda i: relay_sum(order(i)))
     for j in (3, 1):
         for c in w_load(j):
             c.wait()
@@ -409,12 +410,16 @@
         second_hop[c].start()
 
     forward(1)
+    for b in (1, 3):
+        relay_copy(b).start()
     each(2, BLOCKS, lambda i: direct_step(order(i)))
     for c in w_load(0):
         c.wait()
     each(0, BLOCKS, own_step)
     each(0, 2, lambda i: sum_step(order(i)))
     forward(0)
+    for b in (0, 2, 1, 3):
+        direct_copy(b).start()
     each(2, BLOCKS, lambda i: sum_step(order(i)))
 
     for c in (q_load, kpool_load, vpool_load, small[8]):

time: 46.1 us -> 44.9 us (0.974)
  Pallas kernels: 44 us -> 42.9 us
    pallas_call x1, Pallas kernels: 42.1 us -> 41 us  [shards(): pl.pallas_call(kernel, out_shape=(jax.ShapeDtypeStruct((2 * decodes, HEAD...]
where the time goes in v5:
time: 44.9 us; the launch traced here: 44.8 us
  Pallas kernels  42.9 us (96%)
  between operations  1.93 us (4%)
    pallas_call x1, Pallas kernels, shards(): pl.pallas_call(kernel, out_shape=(jax.ShapeDtypeStruct((2 * decodes, HEAD...  41 us
    pallas_call x1, Pallas kernels, shards(): pl.pallas_call(hand_over, out_shape=tuple((jax.ShapeDtypeStruct(a.shape,...  1.9 us

profile of v5, /device:TPU:1, one launch (start us, length us, event | category | flops | bytes accessed | tf_op | source)
XLA Modules:
  0.0 44.8 jit_solution(13278334294816977274)
XLA Ops:
  1.9 41.0 %shard_map.175 = (bf16[128,128]{1,0:T(8,128)(2,1)}, bf16[1920,128]{1,0:T(8,128)(2,1)}, bf16[64,1024]{1,0:T(8,128)(2,1)}) custom-call(bf16[1024,2048]{1,0:T(8,128)(2,1)} %x_hbm.1, bf16[2048,512]{1,0:T(8,128)(2,1)} %wk_hbm.1, bf16[2048,512]{1,0:T(8,128)(2,1)} %wv_hbm.1, bf16[4,64,2048]{2,1,0:T(8,128)(2,1)} %bitcast.8, bf16[512,128]{1,0:T(8,128)(2,1)} %bitcast.9, ...), custom_call_target="tpu_custom_call" | custom-call | tf_op jit(solution)/shard_map/pallas_call | solution.py:636
  42.9 1.9 %shard_map.176 = (bf16[128,128]{1,0:T(8,128)(2,1)}, bf16[1920,128]{1,0:T(8,128)(2,1)}, bf16[64,1024]{1,0:T(8,128)(2,1)}) custom-call(bf16[128,128]{1,0:T(8,128)(2,1)} %get-tuple-element.9.dec, bf16[1920,128]{1,0:T(8,128)(2,1)} %get-tuple-element.10.pre, bf16[64,1024]{1,0:T(8,128)(2,1)} %get-tuple-element.11.att), custom_call_target="tpu_custom_call" | custom-call | tf_op jit(solution)/shard_map/pallas_call | solution.py:725

commit v6 on v5

--- a/solution.py
+++ b/solution.py
@@ -14,6 +14,7 @@
 CHUNKS = 2
 GROUP = 16
 PIECE = 64
+LIMIT = 40 * 1024 * 1024
 MESH = pl.DeviceIdType.MESH
 F32 = jnp.float32
 BF16 = jnp.bfloat16
@@ -58,9 +59,7 @@
     vpool_hbm,
     low_hbm,
     high_hbm,
-    dec_out,
-    pre_out,
-    att_out,
+    out,
     up_ref,
     owner_ref,
     slot_ref,
@@ -104,9 +103,6 @@
     own,
     stage,
     dec,
-    dec_half,
-    pre,
-    att,
     base,
     lens,
     m_s,
@@ -482,7 +478,6 @@
     for b in (0, 2, 1, 3):
         sum_copy(b).start()
 
-    written = []
     sign = jnp.where(iota((1, HEAD), 1) < HALF, -1.0, 1.0)
 
     def rotated(keys, cosine, sine):
@@ -506,10 +501,8 @@
             stage[pl.ds(2 * i * PIECE + 1, PIECE, stride=2), :] = piece[:, HEAD:]
         skip = 2 * PIECE if b == 0 else 0
         begin = 2 * (b * rows - decodes) + skip
-        pre[begin : begin + 2 * rows - skip, :] = stage[skip:, :].astype(BF16)
-        here = pl.ds(begin, 2 * rows - skip)
-        written.append(load(pre.at[here], pre_out.at[here], b))
-        written[-1].start()
+        begin = begin + 2 * decodes
+        out[begin : begin + 2 * rows - skip, :] = stage[skip:, :].astype(BF16)
 
     for k in far_first(tps):
         low_copy(k).wait_recv()
@@ -547,9 +540,7 @@
     values = both[:, HEAD:].astype(BF16).astype(F32)
     dec[pl.ds(0, decodes, stride=2), :] = keys
     dec[pl.ds(1, decodes, stride=2), :] = values
-    dec_half[...] = dec[...].astype(BF16)
-    written.append(load(dec_half, dec_out, BLOCKS))
-    written[-1].start()
+    out[0 : 2 * decodes, :] = dec[...].astype(BF16)
     for i in range(decodes // GROUP):
         key = jnp.concatenate([keys[i * GROUP : (i + 1) * GROUP]] * heads, axis=0)
         value = jnp.concatenate([values[i * GROUP : (i + 1) * GROUP]] * heads, axis=0)
@@ -560,11 +551,8 @@
         share = jnp.exp(score - top)
         result = (o_s[i] * shrink + share * value) / (l_s[i] * shrink + share)
         for g in range(heads):
-            att[i * GROUP : (i + 1) * GROUP, g * HEAD : (g + 1) * HEAD] = result[
-                g * GROUP : (g + 1) * GROUP
-            ].astype(BF16)
-    written.append(load(att, att_out, BLOCKS + 1))
-    written[-1].start()
+            begin = 2 * x.shape[0] + g * decodes + i * GROUP
+            out[begin : begin + GROUP, :] = result[g * GROUP : (g + 1) * GROUP].astype(BF16)
 
     for hop in first_hop + second_hop + back_hop:
         hop.all().wait_send()
@@ -578,21 +566,23 @@
         sum_copy(b).wait_send()
 
     each(0, BLOCKS, sent)
-    for c in written:
+
+
+def hand_over(held, dec_out, pre_out, att_out, sem):
+    decodes = att_out.shape[0]
+    middle = 2 * decodes + pre_out.shape[0]
+    copies = [
+        pltpu.make_async_copy(held.at[pl.ds(0, 2 * decodes)], dec_out, sem.at[0]),
+        pltpu.make_async_copy(held.at[pl.ds(2 * decodes, pre_out.shape[0])], pre_out, sem.at[1]),
+    ]
+    for g in range(att_out.shape[1] // HEAD):
+        source = held.at[pl.ds(middle + g * decodes, decodes)]
+        target = att_out.at[:, pl.ds(g * HEAD, HEAD)]
+        copies.append(pltpu.make_async_copy(source, target, sem.at[2 + g]))
+    for c in copies:
+        c.start()
+    for c in copies:
         c.wait()
-
-
-def hand_over(dec, pre, att, dec_out, pre_out, att_out, pre_held, att_held, dec_held, sem):
-    ways = ((pre, pre_held, pre_out), (att, att_held, att_out), (dec, dec_held, dec_out))
-    fetched = [pltpu.make_async_copy(a, b, sem.at[0, i]) for i, (a, b, _) in enumerate(ways)]
-    written = [pltpu.make_async_copy(b, c, sem.at[1, i]) for i, (_, b, c) in enumerate(ways)]
-    for c in fetched:
-        c.start()
-    for c, e in zip(fetched, written):
-        c.wait()
-        e.start()
-    for e in written:
-        e.wait()
 
 
 def shards(
@@ -624,6 +614,7 @@
     groups = decodes // GROUP
     heads = queries.shape[1] // HEAD
     span = decodes * request_page_table.shape[1] * page
+    vmem = pl.BlockSpec(memory_space=pltpu.VMEM)
     hbm = pl.BlockSpec(memory_space=pltpu.HBM)
     dma = pltpu.SemaphoreType.DMA
 
@@ -633,15 +624,11 @@
     def fl(*shape):
         return pltpu.VMEM(shape, F32)
 
-    decode_kv, prefill_kv, attended = pl.pallas_call(
+    held = pl.pallas_call(
         kernel,
-        out_shape=(
-            jax.ShapeDtypeStruct((2 * decodes, HEAD), BF16),
-            jax.ShapeDtypeStruct((2 * prefills, HEAD), BF16),
-            jax.ShapeDtypeStruct(queries.shape, BF16),
-        ),
+        out_shape=jax.ShapeDtypeStruct((2 * total + decodes * heads, HEAD), BF16),
         in_specs=[hbm] * 16,
-        out_specs=(hbm, hbm, hbm),
+        out_specs=vmem,
         scratch_shapes=[
             bf(2 * adapters * rank, HEAD),
             pltpu.VMEM((1, decodes), jnp.int32),
@@ -683,9 +670,6 @@
             fl(total, 2 * HEAD),
             fl(2 * rows, HEAD),
             fl(2 * decodes, HEAD),
-            bf(2 * decodes, HEAD),
-            bf(2 * prefills, HEAD),
-            bf(*queries.shape),
             fl(16, 2 * HEAD),
             fl(decodes, HEAD),
             fl(groups, GROUP * heads, HEAD),
@@ -702,9 +686,9 @@
             dma((tps,)),
         ],
         compiler_params=pltpu.CompilerParams(
-            collective_id=0, has_side_effects=True, vmem_limit_bytes=60 * 1024 * 1024
+            collective_id=0, has_side_effects=True, vmem_limit_bytes=LIMIT
         ),
-    )(
+    )(*(a if a.size == 1 else pltpu.with_memory_space_constraint(a, pltpu.HBM) for a in (
         normed_input_rows,
         key_projection_weight,
         value_projection_weight,
@@ -721,15 +705,19 @@
         paged_cache_values,
         jnp.asarray(trig(1, 128)),
         jnp.asarray(trig(PIECE, 64)),
-    )
+        )))
     decode_kv, prefill_kv, attended = pl.pallas_call(
         hand_over,
-        out_shape=tuple(jax.ShapeDtypeStruct(a.shape, BF16) for a in (decode_kv, prefill_kv, attended)),
-        in_specs=[hbm] * 3,
+        out_shape=(
+            jax.ShapeDtypeStruct((2 * decodes, HEAD), BF16),
+            jax.ShapeDtypeStruct((2 * prefills, HEAD), BF16),
+            jax.ShapeDtypeStruct(queries.shape, BF16),
+        ),
+        in_specs=[vmem],
         out_specs=(hbm,) * 3,
-        scratch_shapes=[bf(*a.shape) for a in (prefill_kv, attended, decode_kv)] + [dma((2, 3))],
-        compiler_params=pltpu.CompilerParams(vmem_limit_bytes=60 * 1024 * 1024),
-    )(decode_kv, prefill_kv, attended)
+        scratch_shapes=[dma((2 + heads,))],
+        compiler_params=pltpu.CompilerParams(vmem_limit_bytes=LIMIT),
+    )(held)
     return (
         decode_kv.reshape(decodes, 2, HEAD),
         prefill_kv.reshape(prefills, 2, HEAD),

time: 44.9 us -> 43.3 us (0.964)
  Pallas kernels: 42.9 us -> 41.3 us
    pallas_call x2, Pallas kernels: 42.9 us -> 41.3 us  [the longest x1 40.3 us: shards(): pl.pallas_call(kernel, out_shape=jax.ShapeDtypeStruct((2 * total + decode...]
where the time goes in v6:
time: 43.3 us; the launch traced here: 43.2 us
  Pallas kernels  41.3 us (95%)
  between operations  1.93 us (4%)
    pallas_call x1, Pallas kernels, shards(): pl.pallas_call(kernel, out_shape=jax.ShapeDtypeStruct((2 * total + decode...  40.3 us
    pallas_call x1, Pallas kernels, shards(): pl.pallas_call(hand_over, out_shape=(jax.ShapeDtypeStruct((2 * decodes, H...  0.91 us

profile of v6, /device:TPU:1, one launch (start us, length us, event | category | flops | bytes accessed | tf_op | source)
XLA Modules:
  0.0 43.2 jit_solution(10242329188642480758)
XLA Ops:
  1.9 40.3 %shard_map.175.held = bf16[2560,128]{1,0:T(8,128)(2,1)S(1)} custom-call(bf16[1024,2048]{1,0:T(8,128)(2,1)} %x_hbm.1, bf16[2048,512]{1,0:T(8,128)(2,1)} %wk_hbm.1, bf16[2048,512]{1,0:T(8,128)(2,1)} %wv_hbm.1, bf16[4,64,2048]{2,1,0:T(8,128)(2,1)} %bitcast.8, bf16[512,128]{1,0:T(8,128)(2,1)} %bitcast.9, s32[1,64]{1,0:T(1,128)} %bitcast.11, s32[1,64]{1,0:T(1,128)} %bitcast.12, ...), custom_call_target="tpu_custom_call" | custom-call | tf_op jit(solution)/shard_map/pallas_call | solution.py:627
  42.3 0.9 %shard_map.176 = (bf16[128,128]{1,0:T(8,128)(2,1)}, bf16[1920,128]{1,0:T(8,128)(2,1)}, bf16[64,1024]{1,0:T(8,128)(2,1)}) custom-call(bf16[2560,128]{1,0:T(8,128)(2,1)S(1)} %shard_map.175.held), custom_call_target="tpu_custom_call" | custom-call | tf_op jit(solution)/shard_map/pallas_call | solution.py:709

commit v7 on v6

--- a/solution.py
+++ b/solution.py
@@ -9,7 +9,9 @@
 HEAD = 128
 HALF = HEAD // 2
 ROPE_BASE = 500000.0
-PLANE = 8
+CORES = 2
+COLUMNS = 4
+PLANE = CORES * COLUMNS
 BLOCKS = 4
 CHUNKS = 2
 GROUP = 16
@@ -90,6 +92,8 @@
     s4,
     r4,
     uall,
+    uall_other,
+    d_other,
     ug,
     ysend,
     yrecv,
@@ -124,6 +128,8 @@
     planes = lax.axis_size("rep") // PLANE
     z = lax.div(rep, PLANE)
     p = lax.rem(rep, PLANE)
+    column_of = lax.div(p, CORES)
+    core = lax.rem(p, CORES)
     rows = x.shape[0] // BLOCKS
     decodes = q.shape[0]
     slots = 2 * lax.axis_size("rep")
@@ -138,8 +144,14 @@
     def z_of(dd):
         return lax.rem(z + dd, planes)
 
-    def p_of(dd):
-        return lax.rem(p + dd, PLANE)
+    def x_of(dd):
+        return lax.rem(column_of + dd, COLUMNS)
+
+    def at_x(to):
+        return at(z * PLANE + to * CORES + core, t)
+
+    def at_other_core():
+        return at(z * PLANE + column_of * CORES + 1 - core, t)
 
     def t_of(dd):
         return lax.rem(t + dd, tps)
@@ -192,8 +204,9 @@
         c.start()
     for k in far_first(planes):
         pl.semaphore_signal(barrier, inc=1, **at(z_of(k) * PLANE + p, t))
-    for k in far_first(PLANE):
-        pl.semaphore_signal(barrier, inc=1, **at(z * PLANE + p_of(k), t))
+    for k in far_first(COLUMNS):
+        pl.semaphore_signal(barrier, inc=1, **at_x(x_of(k)))
+    pl.semaphore_signal(barrier, inc=1, **at_other_core())
     for k in far_first(tps):
         pl.semaphore_signal(barrier, inc=1, **at(rep, t_of(k)))
     for c in small[3:]:
@@ -227,51 +240,55 @@
     rank_col = jnp.sum(jnp.where(same & before_col, 1.0, 0.0), axis=1, keepdims=True)
     rank_row = jnp.sum(jnp.where(same & before_row, 1.0, 0.0), axis=0, keepdims=True)
 
-    def plane_first(owner, turn):
+    def x_first(owner, turn):
         owner = owner.astype(jnp.int32)
-        return (owner & (PLANE - 1)) * 16 + (owner >> 3) * 2 + turn.astype(jnp.int32)
+        place = ((owner >> 1) & 3) * 32 + (owner >> 3) * 4 + (owner & 1) * 2
+        return place + turn.astype(jnp.int32)
 
     slot_of = iota((slots, decodes), 0)
     placing = (
         one_hot((2.0 * owner_row + rank_row).astype(jnp.int32) == slot_of),
-        one_hot(plane_first(owner_row, rank_row) == slot_of),
+        one_hot(x_first(owner_row, rank_row) == slot_of),
     )
-    placing_back = one_hot(plane_first(owner_col, rank_col) == iota((decodes, slots), 1))
+    placing_back = one_hot(x_first(owner_col, rank_col) == iota((decodes, slots), 1))
     codes = jnp.broadcast_to(column(slot_ref[...].astype(F32)) + 1.0, (decodes, HEAD)).astype(BF16)
 
     head_load.wait()
     for c in range(CHUNKS):
         placed = mm(placing[c], x[0:decodes, c * width : (c + 1) * width]).astype(BF16)
-        s1[c][:, :, 0:width] = placed.reshape(planes, 16, width)
+        s1[c][:, :, 0:width] = placed.reshape(s1[c].shape[:2] + (width,))
     s1a[:, :, width : width + HEAD] = mm(placing[0], codes).astype(BF16).reshape(planes, 16, HEAD)
 
     def copy(source, target, send, recv, where):
         return pltpu.make_async_remote_copy(source, target, send, recv, **where)
 
     class Exchange:
-        def __init__(self, sent, got, me, of, place, send, recv):
-            self.sent, self.got, self.me, self.send, self.recv = sent, got, me, send, recv
-            self.of, self.place = of, place
+        def __init__(self, sent, got, me, of, place, k):
+            self.sent, self.got, self.me, self.of, self.place = sent, got, me, of, place
+            self.send, self.recv, self.count = ex_s.at[k], ex_r.at[k], sent.shape[0]
 
         def start(self):
-            for k in far_first(PLANE):
+            for k in far_first(self.count):
                 to = self.of(k)
                 copy(self.sent.at[to], self.got.at[self.me], self.send, self.recv, self.place(to)).start()
             self.got[self.me] = self.sent[self.me]
 
         def all(self):
-            most = pl.ds(0, PLANE - 1)
+            most = pl.ds(0, self.count - 1)
             return copy(self.sent.at[most], self.got.at[most], self.send, self.recv, self.place(self.of(1)))
 
     def over_z(sent, got, k):
-        return Exchange(sent, got, z, z_of, lambda to: at(to * PLANE + p, t), ex_s.at[k], ex_r.at[k])
-
-    def over_plane(sent, got, k):
-        return Exchange(sent, got, p, p_of, lambda to: at(z * PLANE + to, t), ex_s.at[k], ex_r.at[k])
-
-    first_hop = (over_z(s1a, r1a, 0), over_plane(s1b, r1b, 1))
-    second_hop = (over_plane(s2a, r2a, 2), over_z(s2b, r2b, 3))
-    back_hop = (over_z(s3, r3, 4), over_plane(s4, r4, 5))
+        return Exchange(sent, got, z, z_of, lambda to: at(to * PLANE + p, t), k)
+
+    def over_x(sent, got, k):
+        return Exchange(sent, got, column_of, x_of, at_x, k)
+
+    first_hop = (over_z(s1a, r1a, 0), over_x(s1b, r1b, 1))
+    second_hop = (over_x(s2a, r2a, 2), over_z(s2b, r2b, 3))
+    back_hop = (over_z(s3, r3, 4), over_x(s4, r4, 5))
+
+    down_copy = copy(d_hbm, d_other, ex_s.at[6], ex_r.at[6], at_other_core())
+    both_up_copy = copy(uall, uall_other, ex_s.at[7], ex_r.at[7], at_other_core())
 
     def up_copy(k):
         return pltpu.make_async_remote_copy(
@@ -304,7 +321,7 @@
             sc.at[b], rc.at[b], ys.at[2, b], yr.at[2, b], **at(rep, t_of(ahead(b)))
         )
 
-    pl.semaphore_wait(barrier, planes - 1 + PLANE - 1 + tps - 1)
+    pl.semaphore_wait(barrier, planes - 1 + COLUMNS - 1 + 1 + tps - 1)
     first_hop[0].start()
     first_hop[1].start()
 
@@ -320,6 +337,8 @@
     ug[t] = uall[selected]
     for k in far_first(tps):
         up_copy(k).start()
+    both_up_copy.start()
+    down_copy.start()
 
     lens[...] = jnp.broadcast_to(column(length_ref[...].astype(F32)), (decodes, HEAD))
 
@@ -339,11 +358,10 @@
     base[:, 0:HEAD] = c0 * cb - s0 * sb
     base[:, HEAD:] = s0 * cb + c0 * sb
 
-    swap_out = iota((slots, slots), 0)
-    swap_in = iota((slots, slots), 1)
-    swap = one_hot(
-        swap_in == ((swap_out >> 1) & 7) * 16 + (swap_out >> 4) * 2 + (swap_out & 1)
-    )
+    out_at = iota((slots, slots), 0)
+    in_at = iota((slots, slots), 1)
+    to_x = one_hot(in_at == ((out_at >> 2) & 7) * 16 + (out_at >> 5) * 4 + (out_at & 3))
+    to_z = one_hot(in_at == ((out_at >> 2) & 3) * 32 + (out_at >> 4) * 4 + (out_at & 3))
 
     d_load.wait()
     for c in w_load(2):
@@ -401,8 +419,8 @@
 
     def forward(c):
         first_hop[c].all().wait_recv()
-        moved = mm(swap, first_hop[c].got[...].reshape(slots, -1)).astype(BF16)
-        second_hop[c].sent[...] = moved.reshape(PLANE, 16, -1)
+        moved = mm((to_x, to_z)[c], first_hop[c].got[...].reshape(slots, -1)).astype(BF16)
+        second_hop[c].sent[...] = moved.reshape(second_hop[c].sent.shape)
         second_hop[c].start()
 
     forward(1)
@@ -456,15 +474,22 @@
         l_s[i] = jnp.broadcast_to(jnp.sum(weights, axis=1, keepdims=True), (GROUP * heads, HEAD))
 
     each(0, decodes // GROUP, cached)
-    def factors_of(c):
-        return d[:, :, c * width : (c + 1) * width].reshape(-1, width)
-
+    here_core = ((iota((slots, d.shape[0] * rank), 0) >> 1) & 1) == core
+
+    def reduced(rows_in, c):
+        part = pl.ds(c * width, width)
+        own_part = mt(rows_in, d[:, :, part].reshape(-1, width))
+        other_part = mt(rows_in, d_other[:, :, part].reshape(-1, width))
+        return jnp.where(here_core, own_part, other_part)
+
+    down_copy.wait_recv()
+    both_up_copy.wait_recv()
     second_hop[0].all().wait_recv()
-    got = mm(swap, r2a[...].reshape(slots, -1)).astype(BF16)
-    partial = mt(got[:, 0:width], factors_of(0))
+    got = mm(to_z, r2a[...].reshape(slots, -1)).astype(BF16)
+    partial = reduced(got[:, 0:width], 0)
     code = got[:, width:].astype(F32)
     second_hop[1].all().wait_recv()
-    partial = partial + mt(r2b[...].reshape(slots, width), factors_of(1))
+    partial = partial + reduced(r2b[...].reshape(slots, width), 1)
     lane_slot = (iota((slots, HEAD), 1) >> 6) + 1
     lane_slot = lane_slot.astype(F32)
     low_half = code == lane_slot
@@ -514,13 +539,19 @@
     )
     coarse = wide.astype(BF16)
     fine = (wide - coarse.astype(F32)).astype(BF16)
-    factors = uall[...].reshape(-1, 2 * HEAD)
-    delta = mm(coarse, factors) + mm(fine, factors)
+    both_parts = jnp.concatenate([coarse, fine], axis=0)
+    own_delta = mm(both_parts, uall[...].reshape(-1, 2 * HEAD))
+    other_delta = mm(both_parts, uall_other[...].reshape(-1, 2 * HEAD))
+    delta = jnp.where(
+        here_core[:, 0 : 2 * HEAD],
+        own_delta[0:slots] + own_delta[slots:],
+        other_delta[0:slots] + other_delta[slots:],
+    )
     s3[...] = delta.astype(BF16).reshape(planes, 16, 2 * HEAD)
     back_hop[0].start()
 
     back_hop[0].all().wait_recv()
-    s4[...] = mm(swap, r3[...].reshape(slots, -1)).astype(BF16).reshape(PLANE, 16, -1)
+    s4[...] = mm(to_x, r3[...].reshape(slots, -1)).astype(BF16).reshape(s4.shape)
     back_hop[1].start()
 
     for b in (0, 2, 1, 3):
@@ -556,6 +587,8 @@
 
     for hop in first_hop + second_hop + back_hop:
         hop.all().wait_send()
+    down_copy.wait_send()
+    both_up_copy.wait_send()
     for k in far_first(tps):
         up_copy(k).wait_send()
         low_copy(k).wait_send()
@@ -648,18 +681,20 @@
             bf(span, HEAD),
             bf(span, HEAD),
             bf(planes, 16, part + HEAD),
+            bf(COLUMNS, 32, part),
+            bf(planes, 16, part + HEAD),
+            bf(COLUMNS, 32, part),
+            bf(COLUMNS, 32, part + HEAD),
             bf(planes, 16, part),
-            bf(planes, 16, part + HEAD),
+            bf(COLUMNS, 32, part + HEAD),
             bf(planes, 16, part),
-            bf(PLANE, 16, part + HEAD),
-            bf(PLANE, 16, part),
-            bf(PLANE, 16, part + HEAD),
-            bf(PLANE, 16, part),
-            bf(PLANE, 16, 2 * HEAD),
-            bf(PLANE, 16, 2 * HEAD),
             bf(planes, 16, 2 * HEAD),
             bf(planes, 16, 2 * HEAD),
+            bf(COLUMNS, 32, 2 * HEAD),
+            bf(COLUMNS, 32, 2 * HEAD),
             bf(adapters, rank, 2 * HEAD),
+            bf(adapters, rank, 2 * HEAD),
+            bf(adapters, rank, width),
             bf(tps, rank, 2 * HEAD),
             bf(slots, HEAD),
             bf(tps - 1, slots, HEAD),
@@ -676,8 +711,8 @@
             fl(groups, GROUP * heads, HEAD),
             fl(groups, GROUP * heads, HEAD),
             dma((BLOCKS + 2 * 4 + 4 + 10,)),
-            dma((6,)),
-            dma((6,)),
+            dma((8,)),
+            dma((8,)),
             dma((tps,)),
             dma((tps,)),
             dma((3, BLOCKS)),

time: 43.3 us -> 42 us (0.970)
  the two profiles are of different devices: /device:TPU:1 before, /device:TPU:2 now
where the time goes in v7:
time: 42 us; the launch traced here: 41.9 us
  Pallas kernels  40 us (95%)
  between operations  1.93 us (5%)
    pallas_call x1, Pallas kernels, shards(): pl.pallas_call(kernel, out_shape=jax.ShapeDtypeStruct((2 * total + decode...  39.1 us
    pallas_call x1, Pallas kernels, shards(): pl.pallas_call(hand_over, out_shape=(jax.ShapeDtypeStruct((2 * decodes, H...  0.91 us

profile of v7, /device:TPU:2, one launch (start us, length us, event | category | flops | bytes accessed | tf_op | source)
XLA Modules:
  0.0 41.9 jit_solution(17654752947417913695)
XLA Ops:
  1.9 39.1 %shard_map.175.held = bf16[2560,128]{1,0:T(8,128)(2,1)S(1)} custom-call(bf16[1024,2048]{1,0:T(8,128)(2,1)} %x_hbm.1, bf16[2048,512]{1,0:T(8,128)(2,1)} %wk_hbm.1, bf16[2048,512]{1,0:T(8,128)(2,1)} %wv_hbm.1, bf16[4,64,2048]{2,1,0:T(8,128)(2,1)} %bitcast.8, bf16[512,128]{1,0:T(8,128)(2,1)} %bitcast.9, s32[1,64]{1,0:T(1,128)} %bitcast.11, s32[1,64]{1,0:T(1,128)} %bitcast.12, ...), custom_call_target="tpu_custom_call" | custom-call | tf_op jit(solution)/shard_map/pallas_call | solution.py:660
  41.0 0.9 %shard_map.176 = (bf16[128,128]{1,0:T(8,128)(2,1)}, bf16[1920,128]{1,0:T(8,128)(2,1)}, bf16[64,1024]{1,0:T(8,128)(2,1)}) custom-call(bf16[2560,128]{1,0:T(8,128)(2,1)S(1)} %shard_map.175.held), custom_call_target="tpu_custom_call" | custom-call | tf_op jit(solution)/shard_map/pallas_call | solution.py:744

commit v8 on v7

--- a/solution.py
+++ b/solution.py
@@ -565,6 +565,21 @@
         precision=lax.Precision.HIGHEST,
         preferred_element_type=F32,
     )
+    for hop in first_hop + second_hop + back_hop[0:1]:
+        hop.all().wait_send()
+    down_copy.wait_send()
+    both_up_copy.wait_send()
+    for k in far_first(tps):
+        up_copy(k).wait_send()
+        low_copy(k).wait_send()
+
+    def sent(b):
+        relay_copy(b).wait_send()
+        direct_copy(b).wait_send()
+        sum_copy(b).wait_send()
+
+    each(0, BLOCKS, sent)
+
     back_hop[1].all().wait_recv()
     both = own[0:decodes, :] + mm(placing_back, r4[...].reshape(slots, -1))
     keys = rotated(both[:, 0:HEAD], angles[:, 0:HEAD], angles[:, HEAD:]).astype(BF16).astype(F32)
@@ -584,21 +599,7 @@
         for g in range(heads):
             begin = 2 * x.shape[0] + g * decodes + i * GROUP
             out[begin : begin + GROUP, :] = result[g * GROUP : (g + 1) * GROUP].astype(BF16)
-
-    for hop in first_hop + second_hop + back_hop:
-        hop.all().wait_send()
-    down_copy.wait_send()
-    both_up_copy.wait_send()
-    for k in far_first(tps):
-        up_copy(k).wait_send()
-        low_copy(k).wait_send()
-
-    def sent(b):
-        relay_copy(b).wait_send()
-        direct_copy(b).wait_send()
-        sum_copy(b).wait_send()
-
-    each(0, BLOCKS, sent)
+    back_hop[1].all().wait_send()
 
 
 def hand_over(held, dec_out, pre_out, att_out, sem):

time: 42 us -> 42 us (level)
  no operation moved by 1% of the time
where the time goes in v8:
time: 42 us; the launch traced here: 41.9 us
  Pallas kernels  39.9 us (95%)
  between operations  1.93 us (5%)
    pallas_call x1, Pallas kernels, shards(): pl.pallas_call(kernel, out_shape=jax.ShapeDtypeStruct((2 * total + decode...  39 us
    pallas_call x1, Pallas kernels, shards(): pl.pallas_call(hand_over, out_shape=(jax.ShapeDtypeStruct((2 * decodes, H...  0.91 us

profile of v8, /device:TPU:2, one launch (start us, length us, event | category | flops | bytes accessed | tf_op | source)
XLA Modules:
  0.0 41.9 jit_solution(16446730648485262985)
XLA Ops:
  1.9 39.0 %shard_map.175.held = bf16[2560,128]{1,0:T(8,128)(2,1)S(1)} custom-call(bf16[1024,2048]{1,0:T(8,128)(2,1)} %x_hbm.1, bf16[2048,512]{1,0:T(8,128)(2,1)} %wk_hbm.1, bf16[2048,512]{1,0:T(8,128)(2,1)} %wv_hbm.1, bf16[4,64,2048]{2,1,0:T(8,128)(2,1)} %bitcast.8, bf16[512,128]{1,0:T(8,128)(2,1)} %bitcast.9, s32[1,64]{1,0:T(1,128)} %bitcast.11, s32[1,64]{1,0:T(1,128)} %bitcast.12, ...), custom_call_target="tpu_custom_call" | custom-call | tf_op jit(solution)/shard_map/pallas_call | solution.py:661
  41.0 0.9 %shard_map.176 = (bf16[128,128]{1,0:T(8,128)(2,1)}, bf16[1920,128]{1,0:T(8,128)(2,1)}, bf16[64,1024]{1,0:T(8,128)(2,1)}) custom-call(bf16[2560,128]{1,0:T(8,128)(2,1)S(1)} %shard_map.175.held), custom_call_target="tpu_custom_call" | custom-call | tf_op jit(solution)/shard_map/pallas_call | solution.py:745
